TPU v7x, 512 devices: a whole 4x8x8 slice. The times are simulated.
512 devices in a mesh: pipe: 8 (over y), dp: 64 (over z, x, core).
Axes of the slice: x: 4, y: 8, z: 8, core: 2. Of those that a mesh axis runs over, the one named last changes fastest.
Arguments:
- rollout_rows: bfloat16 [8, 64, 64, 2, 8192], P('pipe', 'dp'), may hold values from -1000 to 1000, as said below
- counts: int32 [8, 64, 64], P('pipe', 'dp'), may hold values from 0 to 2, as said below
- targets: int32 [64, 8, 64], P('dp'), may hold values from 0 to 3071
- final_gain: float32 [8192], replicated, may hold values from 0.5 to 1.5
- lm_head: bfloat16 [8192, 3072], P('dp', 'pipe'), may hold values from -1 to 1
Outputs:
- log_probs: float32 [8, 64, 64], P('pipe', 'dp')
Inputs may be any that keep to these rules, and one draw needn't show every extreme that they name: For every micro-batch and learner the counts over owners sum to 64; every learner receives exactly 2 rows from some owner, and some owners send it nothing. `rollout_rows`: slots k >= counts[p, d, o] hold rows that no learner reads.
All inputs are finite; a program needn't handle non-finite values.
Results may differ from a plain program's by a relative error of at most 0.0011.
Values may be sent and summed in bfloat16 or wider, within the bound.
A program may use at most 64 MiB of HBM per device.

v0:
```python
import jax
import jax.numpy as jnp
from jax import lax
from jax.sharding import PartitionSpec as P


def shifted(block, axis, distance):
    devices = range(lax.axis_size(axis))
    route = [((i - distance) % len(devices), i) for i in devices]
    return lax.ppermute(block, axis, route)


def slice_statistics(normed_rows, wanted, weights, first_column):
    logits = jnp.dot(normed_rows, weights, preferred_element_type=jnp.float32)
    largest = jnp.max(logits, axis=-1)
    exp_total = jnp.sum(jnp.exp(logits - largest[:, None]), axis=-1)
    column_ids = first_column + lax.broadcasted_iota(jnp.int32, logits.shape, 1)
    target_logit = jnp.sum(jnp.where(column_ids == wanted[:, None], logits, 0.0), axis=-1)
    return (largest, exp_total, target_logit)


def body(rollout_rows, counts, targets, final_gain, lm_head):
    owner_slots = rollout_rows[0, 0]
    feature_count = owner_slots.shape[-1]
    holder_count = owner_slots.shape[0]
    slot_count = owner_slots.shape[1]
    arrived = lax.all_to_all(owner_slots, "dp", split_axis=0, concat_axis=0, tiled=True)
    learner_counts = counts[0, 0]
    count_ends = jnp.cumsum(learner_counts)
    count_starts = count_ends - learner_counts
    batch_rows = targets.shape[-1]
    position = jnp.arange(batch_rows, dtype=jnp.int32)
    owner_index = jnp.sum((count_ends[None, :] <= position[:, None]).astype(jnp.int32), axis=-1)
    offset_row = position - jnp.take(count_starts, owner_index)
    learner_rows = jnp.take(
        arrived.reshape(holder_count * slot_count, feature_count),
        owner_index * slot_count + offset_row,
        axis=0,
    )
    widened = learner_rows.astype(jnp.float32)
    scaling = lax.rsqrt(jnp.mean(widened * widened, axis=-1, keepdims=True) + 1e-06)
    normed = (widened * scaling * final_gain).astype(jnp.bfloat16)
    weights = lax.all_gather(lm_head, "dp", axis=0, tiled=True)
    sections = lax.axis_size("pipe")
    section_here = lax.axis_index("pipe")
    first_column = section_here * weights.shape[1]
    wanted_all = targets[0]
    maxima = jnp.zeros((sections, batch_rows), jnp.float32)
    totals = jnp.zeros((sections, batch_rows), jnp.float32)
    target_terms = jnp.zeros((sections, batch_rows), jnp.float32)
    current = normed
    for section_step in range(sections):
        holding = (section_here - section_step) % sections
        wanted = lax.dynamic_index_in_dim(wanted_all, holding, 0, keepdims=False)
        largest, exp_total, target_logit = slice_statistics(current, wanted, weights, first_column)
        maxima = lax.dynamic_update_index_in_dim(maxima, largest, holding, 0)
        totals = lax.dynamic_update_index_in_dim(totals, exp_total, holding, 0)
        target_terms = lax.dynamic_update_index_in_dim(target_terms, target_logit, holding, 0)
        if section_step + 1 < sections:
            current = shifted(current, "pipe", 1)
    maxima, totals, target_terms = (
        lax.all_to_all(maxima, "pipe", split_axis=0, concat_axis=0, tiled=True),
        lax.all_to_all(totals, "pipe", split_axis=0, concat_axis=0, tiled=True),
        lax.all_to_all(target_terms, "pipe", split_axis=0, concat_axis=0, tiled=True),
    )
    overall_max = jnp.max(maxima, axis=0)
    overall_total = jnp.sum(totals * jnp.exp(maxima - overall_max[None, :]), axis=0)
    log_probs = jnp.sum(target_terms, axis=0) - (overall_max + jnp.log(overall_total))
    return log_probs.reshape(1, 1, batch_rows)


def solution(mesh):
    in_specs = (
        P("pipe", "dp", None, None, None),
        P("pipe", "dp", None),
        P("dp", None, None),
        P(),
        P("dp", "pipe"),
    )
    out_specs = P("pipe", "dp", None)
    return jax.shard_map(body, mesh=mesh, in_specs=in_specs, out_specs=out_specs, check_vma=False)
```

profile of v0, /device:TPU:130, one launch (start us, length us, event | category | flops | bytes accessed | tf_op | source)
XLA Modules:
  0.0 314.4 jit_solution(17175567967782775148)
XLA Ops:
  6.5 12.2 %all-to-all-start = ((bf16[64,2,8192]{2,1,0:T(2,128)(2,1)}), bf16[64,2,8192]{2,1,0:T(2,128)(2,1)}, u32[]{:S(2)}, u32[]{:S(2)}) async-start(bf16[64,2,8192]{2,1,0:T(2,128)(2,1)} %bitcast.107), calls=%async_computation | async-start | bytes 4194304 | tf_op jit(solution)/shard_map/all_to_all | solution.py:27
  22.1 49.2 %all-to-all-done = bf16[64,2,8192]{2,1,0:T(2,128)(2,1)} async-done(((bf16[64,2,8192]{2,1,0:T(2,128)(2,1)}), bf16[64,2,8192]{2,1,0:T(2,128)(2,1)}, u32[]{:S(2)}, u32[]{:S(2)}) %all-to-all-start) | async-done | bytes 2097184 | tf_op jit(solution)/shard_map/all_to_all | solution.py:27
  71.3 2.7 reshape.249
  74.0 1.2 gather_fusion.1
  76.1 3.6 %collective-permute-start = (bf16[64,8192]{1,0:T(8,128)(2,1)S(1)}, bf16[64,8192]{1,0:T(8,128)(2,1)S(1)}, u32[]{:S(2)}, u32[]{:S(2)}) collective-permute-start(bf16[64,8192]{1,0:T(8,128)(2,1)S(1)} %fusion.2), channel_id=1, source_target_pairs={{448,0},{0,64},{64,128},{128,192},{192,256},{256,320},{320,384},{3... | collective-permute-start | bytes 3145736 | tf_op jit(solution)/shard_map/ppermute | solution.py:10
  79.7 25.4 %collective-permute-done = bf16[64,8192]{1,0:T(8,128)(2,1)S(1)} collective-permute-done((bf16[64,8192]{1,0:T(8,128)(2,1)S(1)}, bf16[64,8192]{1,0:T(8,128)(2,1)S(1)}, u32[]{:S(2)}, u32[]{:S(2)}) %collective-permute-start) | collective-permute-done | bytes 1048608 | tf_op jit(solution)/shard_map/ppermute | solution.py:10
  105.1 2.1 collective-permute-start.1
  107.2 25.9 %collective-permute-done.1 = bf16[64,8192]{1,0:T(8,128)(2,1)S(1)} collective-permute-done((bf16[64,8192]{1,0:T(8,128)(2,1)S(1)}, bf16[64,8192]{1,0:T(8,128)(2,1)S(1)}, u32[]{:S(2)}, u32[]{:S(2)}) %collective-permute-start.1) | collective-permute-done | bytes 1048608 | tf_op jit(solution)/shard_map/ppermute | solution.py:10
  133.1 1.9 collective-permute-start.2
  135.0 25.2 %collective-permute-done.2 = bf16[64,8192]{1,0:T(8,128)(2,1)S(1)} collective-permute-done((bf16[64,8192]{1,0:T(8,128)(2,1)S(1)}, bf16[64,8192]{1,0:T(8,128)(2,1)S(1)}, u32[]{:S(2)}, u32[]{:S(2)}) %collective-permute-start.2) | collective-permute-done | bytes 1048608 | tf_op jit(solution)/shard_map/ppermute | solution.py:10
  160.2 1.0 copy-done.1
  161.1 1.9 collective-permute-start.3
  163.1 24.3 %collective-permute-done.3 = bf16[64,8192]{1,0:T(8,128)(2,1)S(1)} collective-permute-done((bf16[64,8192]{1,0:T(8,128)(2,1)S(1)}, bf16[64,8192]{1,0:T(8,128)(2,1)S(1)}, u32[]{:S(2)}, u32[]{:S(2)}) %collective-permute-start.3) | collective-permute-done | bytes 1048608 | tf_op jit(solution)/shard_map/ppermute | solution.py:10
  188.3 1.9 collective-permute-start.4
  190.2 23.4 %collective-permute-done.4 = bf16[64,8192]{1,0:T(8,128)(2,1)} collective-permute-done((bf16[64,8192]{1,0:T(8,128)(2,1)S(1)}, bf16[64,8192]{1,0:T(8,128)(2,1)}, u32[]{:S(2)}, u32[]{:S(2)}) %collective-permute-start.4) | collective-permute-done | bytes 1048608 | tf_op jit(solution)/shard_map/ppermute | solution.py:10
  213.6 1.9 collective-permute-start.5
  215.8 22.5 %collective-permute-done.5 = bf16[64,8192]{1,0:T(8,128)(2,1)} collective-permute-done((bf16[64,8192]{1,0:T(8,128)(2,1)}, bf16[64,8192]{1,0:T(8,128)(2,1)}, u32[]{:S(2)}, u32[]{:S(2)}) %collective-permute-start.5) | collective-permute-done | bytes 1048608 | tf_op jit(solution)/shard_map/ppermute | solution.py:10
  238.3 2.1 collective-permute-start.6
  240.4 4.1 %fusion.17 = (f32[64]{0:T(128)S(1)}, f32[64,384]{1,0:T(8,128)S(1)}) fusion(bf16[64,8192]{1,0:T(8,128)(2,1)S(1)} %fusion.2, bf16[8192,384]{1,0:T(8,128)(2,1)} %all-gather.2.cloned.1.call-done), kind=kOutput, calls=%fused_computation.87 | convolution fusion | flops 402677696 | bytes 7438592 | tf_op jit(solution)/shard_map/dot_general | solution.py:14
  245.6 1.2 fusion.19
  247.4 1.2 fusion.20
  249.1 1.2 fusion.21
  250.8 1.2 fusion.22
  252.0 2.4 fusion.23
  255.5 2.4 fusion.16
  258.5 3.5 %collective-permute-done.6 = bf16[64,8192]{1,0:T(8,128)(2,1)} collective-permute-done((bf16[64,8192]{1,0:T(8,128)(2,1)}, bf16[64,8192]{1,0:T(8,128)(2,1)}, u32[]{:S(2)}, u32[]{:S(2)}) %collective-permute-start.6) | collective-permute-done | bytes 1048608 | tf_op jit(solution)/shard_map/ppermute | solution.py:10
  262.0 2.4 fusion.18
  265.0 6.8 %all-to-all-start.2 = ((f32[8,1,64]{2,1,0:T(1,128)}), f32[8,1,64]{2,1,0:T(1,128)S(1)}, u32[]{:S(2)}, u32[]{:S(2)}) async-start(f32[8,1,64]{2,1,0:T(1,128)} %constant_dynamic-update-slice_fusion.8), calls=%async_computation.2 | async-start | bytes 8192 | tf_op jit(solution)/shard_map/all_to_all | solution.py:62
  281.3 7.2 %all-to-all-start.3 = ((f32[8,1,64]{2,1,0:T(1,128)}), f32[8,1,64]{2,1,0:T(1,128)S(1)}, u32[]{:S(2)}, u32[]{:S(2)}) async-start(f32[8,1,64]{2,1,0:T(1,128)} %constant_dynamic-update-slice_fusion), calls=%async_computation.3 | async-start | bytes 8192 | tf_op jit(solution)/shard_map/all_to_all | solution.py:63
  289.1 7.1 %all-to-all-done.3 = f32[8,1,64]{2,1,0:T(1,128)S(1)} async-done(((f32[8,1,64]{2,1,0:T(1,128)}), f32[8,1,64]{2,1,0:T(1,128)S(1)}, u32[]{:S(2)}, u32[]{:S(2)}) %all-to-all-start.3) | async-done | bytes 2080 | tf_op jit(solution)/shard_map/all_to_all | solution.py:63
  296.2 3.2 %all-to-all-start.1 = ((f32[8,1,64]{2,1,0:T(1,128)}), f32[8,1,64]{2,1,0:T(1,128)S(1)}, u32[]{:S(2)}, u32[]{:S(2)}) async-start(f32[8,1,64]{2,1,0:T(1,128)} %constant_dynamic-update-slice_fusion.16), calls=%async_computation.1 | async-start | bytes 8192 | tf_op jit(solution)/shard_map/all_to_all | solution.py:64
  299.5 7.6 %all-to-all-done.1 = f32[8,1,64]{2,1,0:T(1,128)S(1)} async-done(((f32[8,1,64]{2,1,0:T(1,128)}), f32[8,1,64]{2,1,0:T(1,128)S(1)}, u32[]{:S(2)}, u32[]{:S(2)}) %all-to-all-start.1) | async-done | bytes 2080 | tf_op jit(solution)/shard_map/all_to_all | solution.py:64
  (65 shorter events, 20.8 us)
Async XLA Ops:
  6.5 64.7 %all-to-all-start = ((bf16[64,2,8192]{2,1,0:T(2,128)(2,1)}), bf16[64,2,8192]{2,1,0:T(2,128)(2,1)}, u32[]{:S(2)}, u32[]{:S(2)}) async-start(bf16[64,2,8192]{2,1,0:T(2,128)(2,1)} %bitcast.107), calls=%async_computation | async-start | bytes 4194304 | tf_op jit(solution)/shard_map/all_to_all | solution.py:27
  18.8 221.6 %all-gather.2.cloned.1.call-start = ((), (), s32[]{:S(2)}) async-start(), calls=%async_computation.4 | async-start | bytes 6389760 | tf_op jit(solution)/shard_map/all_gather | solution.py:43
  74.0 1.7 copy-start.5
  74.0 141.7 %copy-start.6 = (s32[1,8,64]{2,1,0:T(8,128)S(1)}, s32[1,8,64]{2,1,0:T(8,128)}, u32[]{:S(2)}) copy-start(s32[1,8,64]{2,1,0:T(8,128)} %param.7) | copy-start | bytes 6148
  76.1 29.0 %collective-permute-start = (bf16[64,8192]{1,0:T(8,128)(2,1)S(1)}, bf16[64,8192]{1,0:T(8,128)(2,1)S(1)}, u32[]{:S(2)}, u32[]{:S(2)}) collective-permute-start(bf16[64,8192]{1,0:T(8,128)(2,1)S(1)} %fusion.2), channel_id=1, source_target_pairs={{448,0},{0,64},{64,128},{128,192},{192,256},{256,320},{320,384},{3... | collective-permute-start | bytes 3145736 | tf_op jit(solution)/shard_map/ppermute | solution.py:10
  105.1 28.0 %collective-permute-start.1 = (bf16[64,8192]{1,0:T(8,128)(2,1)S(1)}, bf16[64,8192]{1,0:T(8,128)(2,1)S(1)}, u32[]{:S(2)}, u32[]{:S(2)}) collective-permute-start(bf16[64,8192]{1,0:T(8,128)(2,1)S(1)} %collective-permute-done), channel_id=1, source_target_pairs={{448,0},{0,64},{64,128},{128,192},{192,256},{256,320},{320,384},{3... | collective-permute-start | bytes 3145736 | tf_op jit(solution)/shard_map/ppermute | solution.py:10
  133.1 27.1 %collective-permute-start.2 = (bf16[64,8192]{1,0:T(8,128)(2,1)S(1)}, bf16[64,8192]{1,0:T(8,128)(2,1)S(1)}, u32[]{:S(2)}, u32[]{:S(2)}) collective-permute-start(bf16[64,8192]{1,0:T(8,128)(2,1)S(1)} %collective-permute-done.1), channel_id=1, source_target_pairs={{448,0},{0,64},{64,128},{128,192},{192,256},{256,320},{320,384},{3... | collective-permute-start | bytes 3145736 | tf_op jit(solution)/shard_map/ppermute | solution.py:10
  160.2 1.0 copy-start.1
  161.1 26.2 %collective-permute-start.3 = (bf16[64,8192]{1,0:T(8,128)(2,1)S(1)}, bf16[64,8192]{1,0:T(8,128)(2,1)S(1)}, u32[]{:S(2)}, u32[]{:S(2)}) collective-permute-start(bf16[64,8192]{1,0:T(8,128)(2,1)S(1)} %collective-permute-done.2), channel_id=1, source_target_pairs={{448,0},{0,64},{64,128},{128,192},{192,256},{256,320},{320,384},{3... | collective-permute-start | bytes 3145736 | tf_op jit(solution)/shard_map/ppermute | solution.py:10
  187.3 1.0 copy-start.3
  188.3 25.4 %collective-permute-start.4 = (bf16[64,8192]{1,0:T(8,128)(2,1)S(1)}, bf16[64,8192]{1,0:T(8,128)(2,1)}, u32[]{:S(2)}, u32[]{:S(2)}) collective-permute-start(bf16[64,8192]{1,0:T(8,128)(2,1)S(1)} %collective-permute-done.3), channel_id=1, source_target_pairs={{448,0},{0,64},{64,128},{128,192},{192,256},{256,320},{320,384},{3... | collective-permute-start | bytes 3145736 | tf_op jit(solution)/shard_map/ppermute | solution.py:10
  213.6 24.6 %collective-permute-start.5 = (bf16[64,8192]{1,0:T(8,128)(2,1)}, bf16[64,8192]{1,0:T(8,128)(2,1)}, u32[]{:S(2)}, u32[]{:S(2)}) collective-permute-start(bf16[64,8192]{1,0:T(8,128)(2,1)} %collective-permute-done.4), channel_id=1, source_target_pairs={{448,0},{0,64},{64,128},{128,192},{192,256},{256,320},{320,384},{3... | collective-permute-start | bytes 3145736 | tf_op jit(solution)/shard_map/ppermute | solution.py:10
  238.3 23.7 %collective-permute-start.6 = (bf16[64,8192]{1,0:T(8,128)(2,1)}, bf16[64,8192]{1,0:T(8,128)(2,1)}, u32[]{:S(2)}, u32[]{:S(2)}) collective-permute-start(bf16[64,8192]{1,0:T(8,128)(2,1)} %collective-permute-done.5), channel_id=1, source_target_pairs={{448,0},{0,64},{64,128},{128,192},{192,256},{256,320},{320,384},{3... | collective-permute-start | bytes 3145736 | tf_op jit(solution)/shard_map/ppermute | solution.py:10
  240.4 5.2 %copy-start = (bf16[8192,384]{1,0:T(8,128)(2,1)S(1)}, bf16[8192,384]{1,0:T(8,128)(2,1)}, u32[]{:S(2)}) copy-start(bf16[8192,384]{1,0:T(8,128)(2,1)} %all-gather.2.cloned.1.call-done) | copy-start | bytes 18874372
  245.6 3.5 %copy-start.2 = (bf16[64,8192]{1,0:T(8,128)(2,1)S(1)}, bf16[64,8192]{1,0:T(8,128)(2,1)}, u32[]{:S(2)}) copy-start(bf16[64,8192]{1,0:T(8,128)(2,1)} %copy-done.1) | copy-start | bytes 3145732
  247.4 3.4 %copy-start.4 = (bf16[64,8192]{1,0:T(8,128)(2,1)S(1)}, bf16[64,8192]{1,0:T(8,128)(2,1)}, u32[]{:S(2)}) copy-start(bf16[64,8192]{1,0:T(8,128)(2,1)} %copy-done.3) | copy-start | bytes 3145732
  265.0 16.3 %all-to-all-start.2 = ((f32[8,1,64]{2,1,0:T(1,128)}), f32[8,1,64]{2,1,0:T(1,128)S(1)}, u32[]{:S(2)}, u32[]{:S(2)}) async-start(f32[8,1,64]{2,1,0:T(1,128)} %constant_dynamic-update-slice_fusion.8), calls=%async_computation.2 | async-start | bytes 8192 | tf_op jit(solution)/shard_map/all_to_all | solution.py:62
  281.3 14.9 %all-to-all-start.3 = ((f32[8,1,64]{2,1,0:T(1,128)}), f32[8,1,64]{2,1,0:T(1,128)S(1)}, u32[]{:S(2)}, u32[]{:S(2)}) async-start(f32[8,1,64]{2,1,0:T(1,128)} %constant_dynamic-update-slice_fusion), calls=%async_computation.3 | async-start | bytes 8192 | tf_op jit(solution)/shard_map/all_to_all | solution.py:63
  296.2 10.9 %all-to-all-start.1 = ((f32[8,1,64]{2,1,0:T(1,128)}), f32[8,1,64]{2,1,0:T(1,128)S(1)}, u32[]{:S(2)}, u32[]{:S(2)}) async-start(f32[8,1,64]{2,1,0:T(1,128)} %constant_dynamic-update-slice_fusion.16), calls=%async_computation.1 | async-start | bytes 8192 | tf_op jit(solution)/shard_map/all_to_all | solution.py:64
Sparse Core Ops, SparseCore 0:
  23.0 90.4 all-gather.1
where the time goes:
time: 315 us; the launch traced here: 314 us
  waiting for transfers between devices  215 us (68%)
  starting transfers between devices  45 us (14%)
  local copies, waits for them, and re-layouts  21.8 us (7%)
  matrix products  16 us (5%)
  between operations  13.8 us (4%)
  other arithmetic  3.16 us (1%)
    ppermute x7, waiting for transfers between devices, shifted(): return lax.ppermute(block, axis, route)  150 us
    all_to_all x1, waiting for transfers between devices, body(): lax.all_to_all(owner_slots, 'dp', split_axis=0, concat_axis=0, tiled=True)  49.2 us
    dot_general x8, matrix products, slice_statistics(): logits = jnp.dot(normed_rows, weights, preferred_element_type=jnp.float32)  16 us
    ppermute x7, starting transfers between devices, shifted(): return lax.ppermute(block, axis, route)  15.4 us
    all_to_all x1, starting transfers between devices, body(): lax.all_to_all(owner_slots, 'dp', split_axis=0, concat_axis=0, tiled=True)  12.2 us
    all_to_all x1, waiting for transfers between devices, body(): lax.all_to_all(target_terms, 'pipe', split_axis=0, concat_axis=0, tiled=T...  7.57 us
    all_to_all x1, starting transfers between devices, body(): lax.all_to_all(totals, 'pipe', split_axis=0, concat_axis=0, tiled=True)  7.24 us
    all_to_all x1, waiting for transfers between devices, body(): lax.all_to_all(totals, 'pipe', split_axis=0, concat_axis=0, tiled=True)  7.07 us
  transfers between devices with their start and end apart: 12, of which 10 were waited for; matrix products, arithmetic and copies ran while one was open for 11% of the time, Pallas kernels for 0%

commit v1 on v0

v1 whole, which is shorter than its diff:
```python
import jax
import jax.numpy as jnp
from jax import lax
from jax.experimental import pallas as pl
from jax.experimental.pallas import tpu as pltpu
from jax.sharding import PartitionSpec as P

NX, NY, NZ, NC = 4, 8, 8, 2
ROWS = 128
FEATURES = 8192
COLS = 384
DEPTH = FEATURES // NZ
PIECE = 128
NQ = 4
QD = DEPTH // NQ
NR = 4
RC = ROWS // NR
MESH = pl.DeviceIdType.MESH


def kernel(x_in, w_in, out_ref, xbuf, wbuf, acc, y_send, y_recv, p_send, p_recv, p_own,
           zp_send, zp_recv, zm_send, zm_recv, xr_send, xr_recv, xl_send, xl_recv,
           s_send, s_recv, own_sem, out_sem):
    y = lax.axis_index("pipe")
    dp = lax.axis_index("dp")
    c = lax.rem(dp, 2)
    x = lax.rem(dp // 2, NX)
    z = dp // (2 * NX)

    def at(zz, xx, cc):
        return (zz * NX + xx) * 2 + cc

    right = (y, at(z, lax.rem(x + 1, NX), c))
    left = (y, at(z, lax.rem(x + NX - 1, NX), c))
    sibling = (y, at(z, x, 1 - c))
    up_z = (y, at(lax.rem(z + 1, NZ), x, c))
    down_z = (y, at(lax.rem(z + NZ - 1, NZ), x, c))
    up_y = (lax.rem(y + 1, NY), dp)
    down_y = (lax.rem(y + NY - 1, NY), dp)
    root_dp = z * 8 + y
    me8 = lax.rem(dp, 8)
    dy = lax.rem(y - me8 + NY, NY)

    barrier = pltpu.get_barrier_semaphore()
    for step in range(1, 8):
        pl.semaphore_signal(barrier, inc=1, device_id=(y, z * 8 + lax.rem(me8 + step, 8)), device_id_type=MESH)
    for other in (up_z, down_z, up_y, down_y):
        pl.semaphore_signal(barrier, inc=1, device_id=other, device_id_type=MESH)
    pl.semaphore_wait(barrier, 11)

    def remote(src, dst, send, recv, device):
        return pltpu.make_async_remote_copy(
            src_ref=src, dst_ref=dst, send_sem=send, recv_sem=recv, device_id=device, device_id_type=MESH)

    def shard_copy():
        return remote(w_in, wbuf.at[0, pl.ds(pl.multiple_of(me8 * PIECE, PIECE), PIECE)],
                      p_send.at[0], p_recv.at[me8], (y, root_dp))

    @pl.when(dy != 0)
    def _():
        shard_copy().start()

    def own_shard():
        return pltpu.make_async_copy(
            w_in, wbuf.at[0, pl.ds(pl.multiple_of(me8 * PIECE, PIECE), PIECE)], p_own.at[0])

    @pl.when(dy == 0)
    def _():
        own_shard().start()

    def rows(ref, i):
        return ref.at[pl.ds(i * RC, RC)]

    def x_right(i):
        return remote(rows(x_in, i), rows(xbuf.at[1, 0], i), xr_send.at[i], xr_recv.at[i], right)

    def x_left(i):
        return remote(rows(x_in, i), rows(xbuf.at[3, 0], i), xl_send.at[i], xl_recv.at[i], left)

    def f_right(i):
        return remote(rows(xbuf.at[1, 0], i), rows(xbuf.at[2, 0], i), xr_send.at[NR + i], xr_recv.at[NR + i], right)

    def sib(d, i):
        src = rows(x_in, i) if d == 0 else rows(xbuf.at[d, 0], i)
        return remote(src, rows(xbuf.at[d, 1], i), s_send.at[d, i], s_recv.at[d, i], sibling)

    own = pltpu.make_async_copy(x_in, xbuf.at[0, 0], own_sem.at[0])
    for i in range(NR):
        x_right(i).start()
        x_left(NR - 1 - i).start()
    own.start()
    for i in range(NR):
        sib(0, i).start()

    def chunk(s, q):
        return wbuf.at[s, pl.ds(q * QD, QD)]

    def y_copy(q, device):
        return remote(chunk(0, q), chunk(0, q), y_send.at[q], y_recv.at[q], device)

    def zp(s, q):
        return remote(chunk(s, q), chunk(s + 1, q), zp_send.at[s, q], zp_recv.at[s, q], up_z)

    def zm(s, q):
        return remote(chunk((8 - s) % 8, q), chunk(7 - s, q), zm_send.at[s, q], zm_recv.at[s, q], down_z)

    def p_wait(i):
        remote(w_in, wbuf.at[0, pl.ds(i * PIECE, PIECE)], p_send.at[0], p_recv.at[i], right).wait_recv()

    def sends_p(s, q):
        return s < 3 or (s == 3 and q < NQ // 2)

    def sends_m(s, q):
        return s < 3 or (s == 3 and q >= NQ // 2)

    events = []

    def ev_y(q):
        @pl.when(dy == 0)
        def _():
            for i in range(q * QD // PIECE, (q + 1) * QD // PIECE):
                @pl.when(me8 == i)
                def _():
                    own_shard().wait()

                @pl.when(me8 != i)
                def _():
                    p_wait(i)
            y_copy(q, up_y).start()
            remote(chunk(0, q), chunk(0, q), y_send.at[NQ + q], y_recv.at[q], down_y).start()

        @pl.when(dy != 0)
        def _():
            y_copy(q, up_y).wait_recv()

        @pl.when((dy >= 1) & (dy <= 3))
        def _():
            y_copy(q, up_y).start()

        @pl.when(dy >= 6)
        def _():
            y_copy(q, down_y).start()

        zp(0, q).start()
        zm(0, q).start()

    def ev_zp(s, q):
        zp(s, q).wait_recv()
        if sends_p(s + 1, q):
            zp(s + 1, q).start()

    def ev_zm(s, q):
        zm(s, q).wait_recv()
        if sends_m(s + 1, q):
            zm(s + 1, q).start()

    def ev_right(i):
        x_right(i).wait_recv()
        sib(1, i).start()
        if i < NR // 2:
            f_right(i).start()

    def f_left_copy(i):
        return remote(rows(xbuf.at[3, 0], i), rows(xbuf.at[2, 0], i), xl_send.at[NR + i], xl_recv.at[NR + i], left)

    def ev_left(i):
        x_left(i).wait_recv()
        sib(3, i).start()
        if i >= NR // 2:
            f_left_copy(i).start()

    def ev_opp_right(i):
        f_right(i).wait_recv()
        sib(2, i).start()

    def ev_opp_left(i):
        f_left_copy(i).wait_recv()
        sib(2, i).start()

    wt = 2.15 * QD / 128
    xt = 11.5 * RC / 32
    for q in range(NQ):
        events.append((9 + wt * q, ev_y, (q,)))
    n = 0
    for s in range(4):
        for q in range(NQ):
            if sends_p(s, q):
                events.append((11 + wt * (n + 1), ev_zp, (s, q)))
                n += 1
    n = 0
    for s in range(4):
        for q in range(NQ):
            if sends_m(s, q):
                events.append((11 + wt * (n + 1), ev_zm, (s, q)))
                n += 1
    for i in range(NR):
        events.append((4 + xt * (i + 1), ev_right, (i,)))
        events.append((4 + xt * (i + 1), ev_left, (NR - 1 - i,)))
    for i in range(NR // 2):
        events.append((4 + xt * (NR + i + 1), ev_opp_right, (i,)))
        events.append((4 + xt * (NR + i + 1), ev_opp_left, (NR - 1 - i,)))

    def sib_wait(d):
        for i in range(NR):
            sib(d, i).wait_recv()

    def multiply(ds, sets, first=False):
        for d in ds:
            for s in sets:
                start = pl.multiple_of(lax.rem(z - s + NZ, NZ) * DEPTH, DEPTH)
                for r in range(2):
                    part = jnp.dot(xbuf[d, r, :, pl.ds(start, DEPTH)], wbuf[s],
                                   preferred_element_type=jnp.float32)
                    if first and s == sets[0]:
                        acc[d, r] = part
                    else:
                        acc[d, r] += part

    def stage_a():
        own.wait()
        sib_wait(0)
        multiply((0,), (0, 1, 7), True)

    def stage_b():
        sib_wait(1)
        sib_wait(3)
        multiply((1, 3), (0, 1, 7), True)
        multiply((0, 1, 3), (2, 6))

    def stage_c():
        multiply((0, 1, 3), (3, 5))

    events.append((11 + wt * 2 * NQ + 0.5, stage_a, ()))
    events.append((11 + wt * 3 * NQ + 0.6, stage_b, ()))
    events.append((11 + wt * 3.5 * NQ - wt, stage_c, ()))
    events.sort(key=lambda e: e[0])

    for _, go, given in events:
        go(*given)
    sib_wait(2)
    multiply((0, 1, 3), (4,))
    multiply((2,), tuple(range(8)), True)

    done = pltpu.make_async_copy(acc, out_ref, out_sem.at[0])
    done.start()

    @pl.when(dy != 0)
    def _():
        shard_copy().wait_send()

    for q in range(NQ):
        @pl.when((dy <= 3) | (dy >= 6))
        def _():
            y_copy(q, up_y).wait_send()

        @pl.when(dy == 0)
        def _():
            remote(chunk(0, q), chunk(0, q), y_send.at[NQ + q], y_recv.at[q], down_y).wait_send()
    for s in range(4):
        for q in range(NQ):
            if sends_p(s, q):
                zp(s, q).wait_send()
            if sends_m(s, q):
                zm(s, q).wait_send()
    for i in range(NR):
        x_right(i).wait_send()
        x_left(i).wait_send()
        for d in range(4):
            sib(d, i).wait_send()
    for i in range(NR // 2):
        f_right(i).wait_send()
        f_left_copy(NR - 1 - i).wait_send()
    done.wait()


def group_logits(rows, shard):
    dma = pltpu.SemaphoreType.DMA
    return pl.pallas_call(
        kernel,
        out_shape=jax.ShapeDtypeStruct((4, 2, ROWS, COLS), jnp.float32),
        in_specs=[pl.BlockSpec(memory_space=pl.ANY)] * 2,
        out_specs=pl.BlockSpec(memory_space=pl.ANY),
        scratch_shapes=[
            pltpu.VMEM((4, 2, ROWS, FEATURES), jnp.bfloat16),
            pltpu.VMEM((NZ, DEPTH, COLS), jnp.bfloat16),
            pltpu.VMEM((4, 2, ROWS, COLS), jnp.float32),
            dma((2 * NQ,)), dma((NQ,)), dma((1,)), dma((8,)), dma((1,)),
            dma((4, NQ)), dma((4, NQ)), dma((4, NQ)), dma((4, NQ)),
            dma((2 * NR,)), dma((2 * NR,)), dma((2 * NR,)), dma((2 * NR,)),
            dma((4, NR)), dma((4, NR)), dma((1,)), dma((1,)),
        ],
        compiler_params=pltpu.CompilerParams(
            collective_id=0, has_side_effects=True, vmem_limit_bytes=48 * 2**20),
        cost_estimate=pl.CostEstimate(flops=2 * 1024 * COLS * FEATURES, bytes_accessed=8 * 2**20, transcendentals=0),
    )(rows, shard)


def body(rollout_rows, counts, targets, final_gain, lm_head):
    y = lax.axis_index("pipe")
    dp = lax.axis_index("dp")
    c, x, z = dp % 2, (dp // 2) % NX, dp // (2 * NX)
    widened = rollout_rows[0, 0].astype(jnp.float32)
    scaling = lax.rsqrt(jnp.mean(widened * widened, axis=-1, keepdims=True) + 1e-06)
    normed = (widened * scaling * final_gain).astype(jnp.bfloat16).reshape(ROWS, FEATURES)

    learner_counts = counts[0, 0]
    owners = learner_counts.shape[0]
    ids = jnp.arange(owners, dtype=jnp.int32)
    starts = jnp.sum(jnp.where(ids[None, :] < ids[:, None], learner_counts[None, :], 0), axis=1)
    slot = jnp.arange(2, dtype=jnp.int32)
    place = jnp.where(slot[None, :] < learner_counts[:, None], starts[:, None] + slot[None, :], -1).reshape(-1)
    batch_rows = targets.shape[-1]
    hit = place[:, None] == jnp.arange(batch_rows, dtype=jnp.int32)[None, :]
    mine = lax.dynamic_index_in_dim(targets[0], y, 0, keepdims=False)
    slot_targets = jnp.sum(jnp.where(hit, mine[None, :], 0), axis=1).reshape(owners, 2)
    all_targets = lax.all_gather(slot_targets, "dp", axis=0, tiled=False)

    logits = group_logits(normed, lm_head)

    near = lax.dynamic_slice_in_dim(all_targets, z * 8, 8, axis=1)
    ox = (x + jnp.array([0, 3, 2, 1], jnp.int32)) % NX
    oc = jnp.array([0, 1], jnp.int32) ^ c
    order = (ox[:, None] * 2 + oc[None, :]).reshape(-1)
    pick = (order[:, None] == jnp.arange(8)[None, :]).astype(jnp.int32)
    wanted = jnp.sum(jnp.where(pick[:, None, :, None] == 1, near[None], 0), axis=2).reshape(4, 2, ROWS)
    first_column = (dp % 8) * COLS
    column_ids = first_column + lax.broadcasted_iota(jnp.int32, logits.shape, 3)
    largest = jnp.max(logits, axis=-1)
    exp_total = jnp.sum(jnp.exp(logits - largest[..., None]), axis=-1)
    target_logit = jnp.sum(jnp.where(column_ids == wanted[..., None], logits, 0.0), axis=-1)
    stats = jnp.stack([largest, exp_total, target_logit])
    stats = stats.reshape(3, 8, owners, 2)
    stats = jnp.sum(jnp.where(pick[None, :, :, None, None] == 1, stats[:, :, None], 0.0), axis=1)
    sent = stats.transpose(2, 1, 3, 0).reshape(owners, 48)
    got = lax.all_to_all(sent, "dp", split_axis=0, concat_axis=0, tiled=True)
    got = got.reshape(NZ, 8, 8, 2, 3)
    top = jnp.max(got[..., 0], axis=1)
    total = jnp.sum(got[..., 1] * jnp.exp(got[..., 0] - top[:, None]), axis=1)
    picked = jnp.sum(got[..., 2], axis=1)
    slot_log_probs = (picked - (top + jnp.log(total))).reshape(-1)
    log_probs = jnp.sum(jnp.where(hit, slot_log_probs[:, None], 0.0), axis=0)
    return log_probs.reshape(1, 1, batch_rows)


def solution(mesh):
    in_specs = (
        P("pipe", "dp", None, None, None),
        P("pipe", "dp", None),
        P("dp", None, None),
        P(),
        P("dp", "pipe"),
    )
    out_specs = P("pipe", "dp", None)
    return jax.shard_map(body, mesh=mesh, in_specs=in_specs, out_specs=out_specs, check_vma=False)
```

time: 315 us -> 176 us (0.56)
  the two profiles are of different devices: /device:TPU:130 before, /device:TPU:1 now
where the time goes in v1:
time: 176 us; the launch traced here: 175 us
  Pallas kernels  85.5 us (49%)
  blocking collectives  74.8 us (42%)
  other arithmetic  7.56 us (4%)
  local copies, waits for them, and re-layouts  7.27 us (4%)
    pallas_call x1, Pallas kernels, group_logits(): pl.pallas_call(kernel, out_shape=jax.ShapeDtypeStruct((4, 2, ROWS, COLS),...  85.5 us
    all_gather x1, blocking collectives, body(): all_targets = lax.all_gather(slot_targets, 'dp', axis=0, tiled=False)  51.2 us
    all_to_all x1, blocking collectives, body(): got = lax.all_to_all(sent, 'dp', split_axis=0, concat_axis=0, tiled=True)  23.6 us
    convert_element_type x1, local copies, waits for them, and re-layouts, body(): widened = rollout_rows[0, 0].astype(jnp.float32)  4.53 us

profile of v1, /device:TPU:1, one launch (start us, length us, event | category | flops | bytes accessed | tf_op | source)
XLA Modules:
  0.0 175.4 jit_solution(82409085187660808)
XLA Ops:
  0.0 4.5 %reshape.165 = f32[128,8192]{1,0:T(8,128)} reshape(bf16[1,1,64,2,8192]{4,3,2,1,0:T(2,128)(2,1)} %param.7) | data formatting | bytes 6291456 | tf_op jit(solution)/shard_map/convert_element_type | solution.py:302
  4.6 2.3 %multiply_reduce_fusion = f32[64,2]{1,0:T(8,128)S(1)} fusion(bf16[1,1,64,2,8192]{4,3,2,1,0:T(2,128)(2,1)S(1)} %copy-done.2), kind=kLoop, calls=%fused_computation.1 | loop fusion | flops 3145600 | bytes 2097664 | tf_op jit(solution)/shard_map/reduce_sum | solution.py:303
  6.8 0.1 rsqrt.12
  7.0 0.1 select_reduce_fusion.5
  7.1 0.1 add_select_fusion
  7.2 0.1 select_n.72
  7.4 0.1 select_reduce_fusion.4
  7.4 0.1 all_gather_reshape.3
  7.7 51.2 %all_gather.3 = s32[64,64,2]{1,2,0:T(2,128)S(1)} all-gather(s32[1,64,2]{1,2,0:T(2,128)S(1)} %copy.23), channel_id=1, replica_groups=mesh['pipe'=8,'dp'=64] {'dp'}, dimensions={0}, use_global_device_ids=true | all-gather | bytes 33280 | tf_op jit(solution)/shard_map/all_gather | solution.py:316
  58.8 0.1 constant_dynamic-slice_fusion
  59.1 0.1 add.104
  59.3 0.1 select_reduce_fusion.2
  59.4 0.2 copy.25
  59.6 0.2 eq.76
  59.8 2.7 %multiply_convert_fusion.x_in = bf16[128,8192]{1,0:T(8,128)(2,1)S(1)} fusion(f32[128,8192]{1,0:T(8,128)} %reshape.165, f32[8192]{0:T(1024)S(1)} %copy-done.3, f32[128]{0:T(128)S(1)} %rsqrt.12), kind=kLoop, calls=%fused_computation | loop fusion | flops 3145728 | bytes 6324736 | tf_op jit(solution)/shard_map/convert_element_type | solution.py:304
  62.5 85.5 %shard_map.73 = f32[4,2,128,384]{3,2,1,0:T(8,128)S(1)} custom-call(bf16[128,8192]{1,0:T(8,128)(2,1)S(1)} %multiply_convert_fusion.x_in, bf16[128,384]{1,0:T(8,128)(2,1)S(1)} %copy-done.1), custom_call_target="tpu_custom_call" | custom-call | flops 6442450944 | bytes 8388608 | tf_op jit(solution)/shard_map/pallas_call | solution.py:278
  148.1 0.2 reduce_max.18
  148.3 0.2 stack.12
  148.5 0.7 exponential_reduce_fusion
  149.2 0.2 stack.14
  149.5 0.1 copy.28
  149.6 0.2 stack.13
  149.8 0.1 copy.27
  149.9 0.1 copy.26
  150.1 0.1 select_reduce_fusion.1
  150.3 23.6 %all_to_all.9 = f32[64,1,48]{2,1,0:T(1,128)S(1)} all-to-all(f32[64,1,48]{2,1,0:T(1,128)S(1)} %copy.31), channel_id=1, replica_groups=mesh['pipe'=8,'dp'=64] {'dp'}, dimensions={0} | all-to-all | bytes 24576 | tf_op jit(solution)/shard_map/all_to_all | solution.py:335
  174.0 0.1 reshape.163
  174.2 0.1 slice_reduce_fusion.1
  174.3 0.2 fusion.1
  174.5 0.1 copy.35
  174.6 0.1 sub.40
  174.8 0.6 select_reduce_fusion.3
  (28 shorter events, 0.6 us)
Async XLA Ops:
  0.0 7.3 %copy-start = (s32[1,8,64]{2,1,0:T(8,128)S(1)}, s32[1,8,64]{2,1,0:T(8,128)}, u32[]{:S(2)}) copy-start(s32[1,8,64]{2,1,0:T(8,128)} %param.9) | copy-start | bytes 6148
  0.0 4.5 %copy-start.2 = (bf16[1,1,64,2,8192]{4,3,2,1,0:T(2,128)(2,1)S(1)}, bf16[1,1,64,2,8192]{4,3,2,1,0:T(2,128)(2,1)}, u32[]{:S(2)}) copy-start(bf16[1,1,64,2,8192]{4,3,2,1,0:T(2,128)(2,1)} %param.7) | copy-start | bytes 6291460
  4.5 2.4 %copy-start.4 = (s32[1,1,64]{2,1,0:T(1,128)S(1)}, s32[1,1,64]{2,1,0:T(1,128)}, u32[]{:S(2)}) copy-start(s32[1,1,64]{2,1,0:T(1,128)} %param.8) | copy-start | bytes 772
  4.5 54.5 %copy-start.5 = (s32[4]{0:T(128)S(1)}, s32[4]{0:T(128)}, u32[]{:S(2)}) copy-start(s32[4]{0:T(128)} %constant.96.clone) | copy-start | bytes 52
  4.5 55.2 %copy-start.3 = (f32[8192]{0:T(1024)S(1)}, f32[8192]{0:T(1024)}, u32[]{:S(2)}) copy-start(f32[8192]{0:T(1024)} %param.10) | copy-start | bytes 98308
  59.8 2.7 %copy-start.1 = (bf16[128,384]{1,0:T(8,128)(2,1)S(1)}, bf16[128,384]{1,0:T(8,128)(2,1)}, u32[]{:S(2)}) copy-start(bf16[128,384]{1,0:T(8,128)(2,1)} %w_in.1) | copy-start | bytes 294916

commit v2 on v1

--- a/solution.py
+++ b/solution.py
@@ -18,9 +18,11 @@
 MESH = pl.DeviceIdType.MESH
 
 
-def kernel(x_in, w_in, out_ref, xbuf, wbuf, acc, y_send, y_recv, p_send, p_recv, p_own,
+def kernel(x_in, w_in, counts_ref, targets_ref, gain_ref, out_ref, raw, xbuf, wbuf, acc,
+           messages, near_targets, ring_targets, hits, wanted, turned, stats, ring_stats, slot_out, slot_in,
+           raw_sem, m_send, m_recv, t_send, t_recv, st_send, st_recv, lp_send, lp_recv, y_send, y_recv, p_send, p_recv, p_own,
            zp_send, zp_recv, zm_send, zm_recv, xr_send, xr_recv, xl_send, xl_recv,
-           s_send, s_recv, own_sem, out_sem):
+           s_send, s_recv):
     y = lax.axis_index("pipe")
     dp = lax.axis_index("dp")
     c = lax.rem(dp, 2)
@@ -41,12 +43,22 @@
     me8 = lax.rem(dp, 8)
     dy = lax.rem(y - me8 + NY, NY)
 
+    def raw_copy(i):
+        return pltpu.make_async_copy(rows(x_in, i), rows(raw, i), raw_sem.at[i])
+
+    def rows(ref, i):
+        return ref.at[pl.ds(i * RC, RC)]
+
+    for i in range(NR):
+        raw_copy(i).start()
+
     barrier = pltpu.get_barrier_semaphore()
     for step in range(1, 8):
         pl.semaphore_signal(barrier, inc=1, device_id=(y, z * 8 + lax.rem(me8 + step, 8)), device_id_type=MESH)
-    for other in (up_z, down_z, up_y, down_y):
+        pl.semaphore_signal(barrier, inc=1, device_id=(y, lax.rem(dp + 8 * step, 64)), device_id_type=MESH)
+    for other in (up_y, down_y):
         pl.semaphore_signal(barrier, inc=1, device_id=other, device_id_type=MESH)
-    pl.semaphore_wait(barrier, 11)
+    pl.semaphore_wait(barrier, 16)
 
     def remote(src, dst, send, recv, device):
         return pltpu.make_async_remote_copy(
@@ -68,29 +80,104 @@
     def _():
         own_shard().start()
 
-    def rows(ref, i):
-        return ref.at[pl.ds(i * RC, RC)]
-
     def x_right(i):
-        return remote(rows(x_in, i), rows(xbuf.at[1, 0], i), xr_send.at[i], xr_recv.at[i], right)
+        return remote(rows(xbuf.at[0, 0], i), rows(xbuf.at[1, 0], i), xr_send.at[i], xr_recv.at[i], right)
 
     def x_left(i):
-        return remote(rows(x_in, i), rows(xbuf.at[3, 0], i), xl_send.at[i], xl_recv.at[i], left)
+        return remote(rows(xbuf.at[0, 0], i), rows(xbuf.at[3, 0], i), xl_send.at[i], xl_recv.at[i], left)
 
     def f_right(i):
         return remote(rows(xbuf.at[1, 0], i), rows(xbuf.at[2, 0], i), xr_send.at[NR + i], xr_recv.at[NR + i], right)
 
     def sib(d, i):
-        src = rows(x_in, i) if d == 0 else rows(xbuf.at[d, 0], i)
-        return remote(src, rows(xbuf.at[d, 1], i), s_send.at[d, i], s_recv.at[d, i], sibling)
-
-    own = pltpu.make_async_copy(x_in, xbuf.at[0, 0], own_sem.at[0])
-    for i in range(NR):
-        x_right(i).start()
-        x_left(NR - 1 - i).start()
-    own.start()
+        return remote(rows(xbuf.at[d, 0], i), rows(xbuf.at[d, 1], i), s_send.at[d, i], s_recv.at[d, i], sibling)
+
+    def normalise(i):
+        for b in range(i * RC, (i + 1) * RC, 16):
+            here = pl.ds(b, 16)
+
+            def add(j, total):
+                v = raw[here, pl.ds(pl.multiple_of(j * 1024, 1024), 1024)].astype(jnp.float32)
+                v = v * v
+                for n in range(8):
+                    total = total + v[:, n * 128:(n + 1) * 128]
+                return total
+
+            total = lax.fori_loop(0, FEATURES // 1024, add, jnp.zeros((16, 128), jnp.float32))
+            scaling = lax.rsqrt(jnp.sum(total, axis=-1, keepdims=True) / FEATURES + 1e-06)
+
+            def put(j, carry):
+                lanes = pl.ds(pl.multiple_of(j * 1024, 1024), 1024)
+                v = raw[here, lanes].astype(jnp.float32)
+                xbuf[0, 0, here, lanes] = (v * scaling * gain_ref[:, lanes]).astype(jnp.bfloat16)
+                return carry
+
+            lax.fori_loop(0, FEATURES // 1024, put, 0)
+
+    for n in range(NR // 2):
+        for i in (n, NR - 1 - n):
+            raw_copy(i).wait()
+            normalise(i)
+        x_right(n).start()
+        x_left(NR - 1 - n).start()
+    for n in range(NR // 2, NR):
+        x_right(n).start()
+        x_left(NR - 1 - n).start()
     for i in range(NR):
         sib(0, i).start()
+
+    def m_copy(j):
+        return remote(messages.at[lax.rem(z + j, NZ)], near_targets.at[j], m_send.at[j], m_recv.at[j],
+                      (y, lax.rem(dp + 8 * j, 64)))
+
+    def ring(j):
+        return (y, z * 8 + lax.rem(me8 + j, 8))
+
+    def t_copy(j):
+        return remote(ring_targets.at[0], ring_targets.at[j], t_send.at[j], t_recv.at[j], ring(j))
+
+    def ev_targets():
+        held = counts_ref[...].astype(jnp.float32)
+        mine = targets_ref[0, pl.ds(y, 1), :].astype(jnp.float32)
+        lane = lax.broadcasted_iota(jnp.int32, (64, 64), 1)
+        row = lax.broadcasted_iota(jnp.int32, (64, 64), 0)
+        start = jnp.sum(jnp.where(lane < row, held, 0.0), axis=1, keepdims=True)
+        number = jnp.sum(jnp.where(lane == row, held, 0.0), axis=1, keepdims=True)
+        place = lax.broadcasted_iota(jnp.int32, (64, 128), 1)
+        made = jnp.zeros((64, 128), jnp.float32)
+        for k in range(2):
+            at_row = jnp.where(number > k, start + k, -1.0)
+            hit = lane.astype(jnp.float32) == at_row
+            hits[k] = jnp.where(hit, 1.0, 0.0)
+            target = jnp.sum(jnp.where(hit, mine, 0.0), axis=1, keepdims=True)
+            made = made + jnp.where(place == 2 * dp + k, target, 0.0)
+        messages[...] = made.reshape(NZ, 8, 128)
+        for j in range(1, 8):
+            m_copy(j).start()
+
+    def ev_near():
+        total = messages[z]
+        for j in range(1, 8):
+            m_copy(j).wait_recv()
+            total = total + near_targets[j]
+        ring_targets[0] = total
+        for j in range(1, 8):
+            t_copy(j).start()
+
+    def owner_of(d, r):
+        return lax.rem(x + (NX - d), NX) * 2 + (c if r == 0 else 1 - c)
+
+    def ev_wanted():
+        total = ring_targets[0]
+        for j in range(1, 8):
+            t_copy(j).wait_recv()
+            total = total + ring_targets[j]
+        wanted[...] = total
+        turned[...] = jnp.zeros((128, 128), jnp.float32)
+        for d in range(4):
+            for r in range(2):
+                turned[2 * d + r:2 * d + r + 1, :] = wanted[pl.ds(owner_of(d, r), 1), :]
+        turned[...] = turned[...].T
 
     def chunk(s, q):
         return wbuf.at[s, pl.ds(q * QD, QD)]
@@ -217,7 +304,6 @@
                         acc[d, r] += part
 
     def stage_a():
-        own.wait()
         sib_wait(0)
         multiply((0,), (0, 1, 7), True)
 
@@ -233,6 +319,7 @@
     events.append((11 + wt * 2 * NQ + 0.5, stage_a, ()))
     events.append((11 + wt * 3 * NQ + 0.6, stage_b, ()))
     events.append((11 + wt * 3.5 * NQ - wt, stage_c, ()))
+    events += [(6, ev_targets, ()), (16, ev_near, ()), (22, ev_wanted, ())]
     events.sort(key=lambda e: e[0])
 
     for _, go, given in events:
@@ -241,8 +328,58 @@
     multiply((0, 1, 3), (4,))
     multiply((2,), tuple(range(8)), True)
 
-    done = pltpu.make_async_copy(acc, out_ref, out_sem.at[0])
-    done.start()
+    column = (lax.broadcasted_iota(jnp.int32, (ROWS, COLS), 1) + me8 * COLS).astype(jnp.float32)
+    place = lax.broadcasted_iota(jnp.int32, (ROWS, 128), 1)
+    gathered = jnp.zeros((ROWS, 128), jnp.float32)
+    for d in range(4):
+        for r in range(2):
+            n = 2 * d + r
+            logits = acc[d, r]
+            largest = jnp.max(logits, axis=1, keepdims=True)
+            exp_total = jnp.sum(jnp.exp(logits - largest), axis=1, keepdims=True)
+            target = jnp.sum(jnp.where(column == turned[:, n:n + 1], logits, 0.0), axis=1, keepdims=True)
+            for which, v in enumerate((largest, exp_total, target)):
+                gathered = jnp.where(place == 8 * which + n, v, gathered)
+    turned[...] = gathered.T
+    for d in range(4):
+        for r in range(2):
+            for which in range(3):
+                n = 8 * which + 2 * d + r
+                stats[which, pl.ds(owner_of(d, r), 1), :] = turned[n:n + 1, :]
+
+    def st_copy(j):
+        return remote(stats, ring_stats.at[j], st_send.at[j], st_recv.at[j], ring(j))
+
+    for j in range(1, 8):
+        st_copy(j).start()
+    for j in range(1, 8):
+        st_copy(j).wait_recv()
+    parts = [stats[...]] + [ring_stats[j] for j in range(1, 8)]
+    top = parts[0][0]
+    for part in parts[1:]:
+        top = jnp.maximum(top, part[0])
+    total = jnp.zeros((8, 128), jnp.float32)
+    picked = jnp.zeros((8, 128), jnp.float32)
+    for part in parts:
+        total = total + part[1] * jnp.exp(part[0] - top)
+        picked = picked + part[2]
+    slot_out[...] = picked - (top + jnp.log(total))
+
+    def lp_copy(j):
+        return remote(slot_out, slot_in.at[z], lp_send.at[j], lp_recv.at[j], (y, lax.rem(dp + 8 * j, 64)))
+
+    for j in range(1, 8):
+        lp_copy(j).start()
+    slot_in[z] = slot_out[...]
+    for j in range(1, 8):
+        source = lax.rem(z + NZ - j, NZ)
+        remote(slot_out, slot_in.at[source], lp_send.at[j], lp_recv.at[j], up_z).wait_recv()
+    slots = slot_in[...].reshape(64, 128)
+    result = jnp.zeros((1, 64), jnp.float32)
+    for k in range(2):
+        value = jnp.sum(jnp.where(place[:64] == 2 * dp + k, slots, 0.0), axis=1, keepdims=True)
+        result = result + jnp.sum(jnp.where(hits[k] > 0.5, value, 0.0), axis=0, keepdims=True)
+    out_ref[...] = result
 
     @pl.when(dy != 0)
     def _():
@@ -270,76 +407,45 @@
     for i in range(NR // 2):
         f_right(i).wait_send()
         f_left_copy(NR - 1 - i).wait_send()
-    done.wait()
-
-
-def group_logits(rows, shard):
+    for j in range(1, 8):
+        m_copy(j).wait_send()
+        t_copy(j).wait_send()
+        st_copy(j).wait_send()
+        lp_copy(j).wait_send()
+
+
+def body(rollout_rows, counts, targets, final_gain, lm_head):
+    rows = lax.optimization_barrier(rollout_rows.reshape(ROWS, FEATURES))
     dma = pltpu.SemaphoreType.DMA
-    return pl.pallas_call(
+    vmem = pl.BlockSpec(memory_space=pltpu.VMEM)
+    hbm = pl.BlockSpec(memory_space=pl.ANY)
+    tile = (8, 128)
+    f32 = jnp.float32
+    log_probs = pl.pallas_call(
         kernel,
-        out_shape=jax.ShapeDtypeStruct((4, 2, ROWS, COLS), jnp.float32),
-        in_specs=[pl.BlockSpec(memory_space=pl.ANY)] * 2,
-        out_specs=pl.BlockSpec(memory_space=pl.ANY),
+        out_shape=jax.ShapeDtypeStruct((1, 64), f32),
+        in_specs=[hbm, hbm, vmem, vmem, vmem],
+        out_specs=vmem,
         scratch_shapes=[
+            pltpu.VMEM((ROWS, FEATURES), jnp.bfloat16),
             pltpu.VMEM((4, 2, ROWS, FEATURES), jnp.bfloat16),
             pltpu.VMEM((NZ, DEPTH, COLS), jnp.bfloat16),
-            pltpu.VMEM((4, 2, ROWS, COLS), jnp.float32),
+            pltpu.VMEM((4, 2, ROWS, COLS), f32),
+            pltpu.VMEM((NZ, *tile), f32), pltpu.VMEM((NZ, *tile), f32), pltpu.VMEM((8, *tile), f32),
+            pltpu.VMEM((2, 64, 64), f32), pltpu.VMEM(tile, f32), pltpu.VMEM((128, 128), f32),
+            pltpu.VMEM((3, *tile), f32), pltpu.VMEM((8, 3, *tile), f32),
+            pltpu.VMEM(tile, f32), pltpu.VMEM((NZ, *tile), f32),
+            dma((NR,)), dma((8,)), dma((8,)), dma((8,)), dma((8,)), dma((8,)), dma((8,)), dma((8,)), dma((8,)),
             dma((2 * NQ,)), dma((NQ,)), dma((1,)), dma((8,)), dma((1,)),
             dma((4, NQ)), dma((4, NQ)), dma((4, NQ)), dma((4, NQ)),
             dma((2 * NR,)), dma((2 * NR,)), dma((2 * NR,)), dma((2 * NR,)),
-            dma((4, NR)), dma((4, NR)), dma((1,)), dma((1,)),
+            dma((4, NR)), dma((4, NR)),
         ],
         compiler_params=pltpu.CompilerParams(
             collective_id=0, has_side_effects=True, vmem_limit_bytes=48 * 2**20),
         cost_estimate=pl.CostEstimate(flops=2 * 1024 * COLS * FEATURES, bytes_accessed=8 * 2**20, transcendentals=0),
-    )(rows, shard)
-
-
-def body(rollout_rows, counts, targets, final_gain, lm_head):
-    y = lax.axis_index("pipe")
-    dp = lax.axis_index("dp")
-    c, x, z = dp % 2, (dp // 2) % NX, dp // (2 * NX)
-    widened = rollout_rows[0, 0].astype(jnp.float32)
-    scaling = lax.rsqrt(jnp.mean(widened * widened, axis=-1, keepdims=True) + 1e-06)
-    normed = (widened * scaling * final_gain).astype(jnp.bfloat16).reshape(ROWS, FEATURES)
-
-    learner_counts = counts[0, 0]
-    owners = learner_counts.shape[0]
-    ids = jnp.arange(owners, dtype=jnp.int32)
-    starts = jnp.sum(jnp.where(ids[None, :] < ids[:, None], learner_counts[None, :], 0), axis=1)
-    slot = jnp.arange(2, dtype=jnp.int32)
-    place = jnp.where(slot[None, :] < learner_counts[:, None], starts[:, None] + slot[None, :], -1).reshape(-1)
-    batch_rows = targets.shape[-1]
-    hit = place[:, None] == jnp.arange(batch_rows, dtype=jnp.int32)[None, :]
-    mine = lax.dynamic_index_in_dim(targets[0], y, 0, keepdims=False)
-    slot_targets = jnp.sum(jnp.where(hit, mine[None, :], 0), axis=1).reshape(owners, 2)
-    all_targets = lax.all_gather(slot_targets, "dp", axis=0, tiled=False)
-
-    logits = group_logits(normed, lm_head)
-
-    near = lax.dynamic_slice_in_dim(all_targets, z * 8, 8, axis=1)
-    ox = (x + jnp.array([0, 3, 2, 1], jnp.int32)) % NX
-    oc = jnp.array([0, 1], jnp.int32) ^ c
-    order = (ox[:, None] * 2 + oc[None, :]).reshape(-1)
-    pick = (order[:, None] == jnp.arange(8)[None, :]).astype(jnp.int32)
-    wanted = jnp.sum(jnp.where(pick[:, None, :, None] == 1, near[None], 0), axis=2).reshape(4, 2, ROWS)
-    first_column = (dp % 8) * COLS
-    column_ids = first_column + lax.broadcasted_iota(jnp.int32, logits.shape, 3)
-    largest = jnp.max(logits, axis=-1)
-    exp_total = jnp.sum(jnp.exp(logits - largest[..., None]), axis=-1)
-    target_logit = jnp.sum(jnp.where(column_ids == wanted[..., None], logits, 0.0), axis=-1)
-    stats = jnp.stack([largest, exp_total, target_logit])
-    stats = stats.reshape(3, 8, owners, 2)
-    stats = jnp.sum(jnp.where(pick[None, :, :, None, None] == 1, stats[:, :, None], 0.0), axis=1)
-    sent = stats.transpose(2, 1, 3, 0).reshape(owners, 48)
-    got = lax.all_to_all(sent, "dp", split_axis=0, concat_axis=0, tiled=True)
-    got = got.reshape(NZ, 8, 8, 2, 3)
-    top = jnp.max(got[..., 0], axis=1)
-    total = jnp.sum(got[..., 1] * jnp.exp(got[..., 0] - top[:, None]), axis=1)
-    picked = jnp.sum(got[..., 2], axis=1)
-    slot_log_probs = (picked - (top + jnp.log(total))).reshape(-1)
-    log_probs = jnp.sum(jnp.where(hit, slot_log_probs[:, None], 0.0), axis=0)
-    return log_probs.reshape(1, 1, batch_rows)
+    )(rows, lm_head, counts[0], targets, final_gain.reshape(1, FEATURES))
+    return log_probs.reshape(1, 1, 64)
 
 
 def solution(mesh):

time: 176 us -> 131 us (0.74)
  blocking collectives: 74.8 us -> 0 us
  Pallas kernels: 85.5 us -> 125 us
  other arithmetic: 7.56 us -> 0 us
  local copies, waits for them, and re-layouts: 7.27 us -> 3.31 us
    all_gather x1 -> x0, blocking collectives: 51.2 us -> none  [body(): all_targets = lax.all_gather(slot_targets, 'dp', axis=0, tiled=False)]
    pallas_call x1, Pallas kernels: 85.5 us -> 125 us  [body(): pl.pallas_call(kernel, out_shape=jax.ShapeDtypeStruct((1, 64), f32), in_s...]
    all_to_all x1 -> x0, blocking collectives: 23.6 us -> none  [body(): got = lax.all_to_all(sent, 'dp', split_axis=0, concat_axis=0, tiled=True)]
    convert_element_type x1 -> x0, local copies, waits for them, and re-layouts: 4.53 us -> none  [body(): widened = rollout_rows[0, 0].astype(jnp.float32)]
    reduce_sum x8 -> x0, other arithmetic: 4.19 us -> none  [the longest x1 2.25 us: body(): jnp.mean(widened * widened, axis=-1, keepdims=True) + 1e-06]
    convert_element_type x1 -> x0, other arithmetic: 2.73 us -> none  [body(): (widened * scaling * final_gain).astype(jnp.bfloat16)]
    reshape x1, local copies, waits for them, and re-layouts: 0.12 us -> 2.78 us  [body(): rows = lax.optimization_barrier(rollout_rows.reshape(ROWS, FEATURES))]
where the time goes in v2:
time: 131 us; the launch traced here: 129 us
  Pallas kernels  125 us (95%)
  local copies, waits for them, and re-layouts  3.31 us (3%)
    pallas_call x1, Pallas kernels, body(): pl.pallas_call(kernel, out_shape=jax.ShapeDtypeStruct((1, 64), f32), in_s...  125 us
    reshape x1, local copies, waits for them, and re-layouts, body(): rows = lax.optimization_barrier(rollout_rows.reshape(ROWS, FEATURES))  2.78 us

profile of v2, /device:TPU:1, one launch (start us, length us, event | category | flops | bytes accessed | tf_op | source)
XLA Modules:
  0.0 128.7 jit_solution(10779443196641848403)
XLA Ops:
  0.0 0.0 copy-start
  0.0 0.0 copy-start.1
  0.0 0.0 copy-start.2
  0.0 0.0 copy-start.3
  0.0 2.8 %reshape.9.x_in = bf16[128,8192]{1,0:T(8,128)(2,1)S(1)} reshape(bf16[1,1,64,2,8192]{4,3,2,1,0:T(2,128)(2,1)} %param.5) | data formatting | bytes 4194304 | tf_op jit(solution)/shard_map/reshape | solution.py:418
  2.8 0.0 copy-done
  2.8 0.0 copy-done.1
  2.8 0.0 copy-done.2
  2.8 0.0 copy-done.3
  2.8 125.3 %shard_map.55 = f32[1,64]{1,0:T(1,128)S(1)} custom-call(bf16[128,8192]{1,0:T(8,128)(2,1)S(1)} %reshape.9.x_in, bf16[128,384]{1,0:T(8,128)(2,1)S(1)} %copy-done, s32[1,64]{1,0:T(1,128)S(1)} %bitcast.4, s32[1,8,64]{2,1,0:T(8,128)S(1)} %copy-done.2, f32[1,8192]{1,0:T(1,128)S(1)} %bitcast.3), custom_call_target="tpu_custom_call" | custom-call | flops 6442450944 | bytes 8388608 | tf_op jit(solution)/shard_map/pallas_call | solution.py:424
  128.2 0.5 copy.7
Async XLA Ops:
  0.0 2.8 %copy-start = (bf16[128,384]{1,0:T(8,128)(2,1)S(1)}, bf16[128,384]{1,0:T(8,128)(2,1)}, u32[]{:S(2)}) copy-start(bf16[128,384]{1,0:T(8,128)(2,1)} %w_in.1) | copy-start | bytes 294916
  0.0 2.8 %copy-start.1 = (f32[8192]{0:T(1024)S(1)}, f32[8192]{0:T(1024)}, u32[]{:S(2)}) copy-start(f32[8192]{0:T(1024)} %param.8) | copy-start | bytes 98308
  0.0 2.8 %copy-start.2 = (s32[1,8,64]{2,1,0:T(8,128)S(1)}, s32[1,8,64]{2,1,0:T(8,128)}, u32[]{:S(2)}) copy-start(s32[1,8,64]{2,1,0:T(8,128)} %targets_ref.1) | copy-start | bytes 6148
  0.0 2.8 %copy-start.3 = (s32[1,1,64]{2,1,0:T(1,128)S(1)}, s32[1,1,64]{2,1,0:T(1,128)}, u32[]{:S(2)}) copy-start(s32[1,1,64]{2,1,0:T(1,128)} %param.6) | copy-start | bytes 772

commit v3 on v2

--- a/solution.py
+++ b/solution.py
@@ -11,15 +11,15 @@
 COLS = 384
 DEPTH = FEATURES // NZ
 PIECE = 128
-NQ = 4
-QD = DEPTH // NQ
+NK = 4
+PART = COLS // NK
 NR = 4
 RC = ROWS // NR
 MESH = pl.DeviceIdType.MESH
 
 
-def kernel(x_in, w_in, counts_ref, targets_ref, gain_ref, out_ref, raw, xbuf, wbuf, acc,
-           messages, near_targets, ring_targets, hits, wanted, turned, stats, ring_stats, slot_out, slot_in,
+def kernel(x_in, w_in, counts_ref, targets_ref, gain_ref, out_ref, raw, flipped, xbuf, wbuf, acc,
+           messages, near_targets, ring_targets, hits, wanted, turned, noted, stats, ring_stats, slot_out, slot_in,
            raw_sem, m_send, m_recv, t_send, t_recv, st_send, st_recv, lp_send, lp_recv, y_send, y_recv, p_send, p_recv, p_own,
            zp_send, zp_recv, zm_send, zm_recv, xr_send, xr_recv, xl_send, xl_recv,
            s_send, s_recv):
@@ -39,9 +39,8 @@
     down_z = (y, at(lax.rem(z + NZ - 1, NZ), x, c))
     up_y = (lax.rem(y + 1, NY), dp)
     down_y = (lax.rem(y + NY - 1, NY), dp)
-    root_dp = z * 8 + y
     me8 = lax.rem(dp, 8)
-    dy = lax.rem(y - me8 + NY, NY)
+    keeper = lax.rem(y, 2) == c
 
     def raw_copy(i):
         return pltpu.make_async_copy(rows(x_in, i), rows(raw, i), raw_sem.at[i])
@@ -58,27 +57,34 @@
         pl.semaphore_signal(barrier, inc=1, device_id=(y, lax.rem(dp + 8 * step, 64)), device_id_type=MESH)
     for other in (up_y, down_y):
         pl.semaphore_signal(barrier, inc=1, device_id=other, device_id_type=MESH)
+    flipped[...] = w_in[...].astype(jnp.float32).T.astype(jnp.bfloat16)
     pl.semaphore_wait(barrier, 16)
 
     def remote(src, dst, send, recv, device):
         return pltpu.make_async_remote_copy(
             src_ref=src, dst_ref=dst, send_sem=send, recv_sem=recv, device_id=device, device_id_type=MESH)
 
-    def shard_copy():
-        return remote(w_in, wbuf.at[0, pl.ds(pl.multiple_of(me8 * PIECE, PIECE), PIECE)],
-                      p_send.at[0], p_recv.at[me8], (y, root_dp))
-
-    @pl.when(dy != 0)
-    def _():
-        shard_copy().start()
+    def shard_copy(step):
+        other = lax.rem(x + step, NX)
+        return remote(flipped.at[pl.ds(pl.multiple_of(other * PART, PART), PART)],
+                      wbuf.at[0, pl.ds(0, PART), pl.ds(pl.multiple_of(me8 * PIECE, PIECE), PIECE)],
+                      p_send.at[step], p_recv.at[me8], (y, at(z, other, lax.rem(y, 2))))
 
     def own_shard():
         return pltpu.make_async_copy(
-            w_in, wbuf.at[0, pl.ds(pl.multiple_of(me8 * PIECE, PIECE), PIECE)], p_own.at[0])
-
-    @pl.when(dy == 0)
+            flipped.at[pl.ds(pl.multiple_of(x * PART, PART), PART)],
+            wbuf.at[0, pl.ds(0, PART), pl.ds(pl.multiple_of(me8 * PIECE, PIECE), PIECE)], p_own.at[0])
+
+    for step in (2, 1, 3):
+        shard_copy(step).start()
+
+    @pl.when(keeper)
     def _():
         own_shard().start()
+
+    @pl.when(jnp.logical_not(keeper))
+    def _():
+        shard_copy(0).start()
 
     def x_right(i):
         return remote(rows(xbuf.at[0, 0], i), rows(xbuf.at[1, 0], i), xr_send.at[i], xr_recv.at[i], right)
@@ -113,18 +119,6 @@
                 return carry
 
             lax.fori_loop(0, FEATURES // 1024, put, 0)
-
-    for n in range(NR // 2):
-        for i in (n, NR - 1 - n):
-            raw_copy(i).wait()
-            normalise(i)
-        x_right(n).start()
-        x_left(NR - 1 - n).start()
-    for n in range(NR // 2, NR):
-        x_right(n).start()
-        x_left(NR - 1 - n).start()
-    for i in range(NR):
-        sib(0, i).start()
 
     def m_copy(j):
         return remote(messages.at[lax.rem(z + j, NZ)], near_targets.at[j], m_send.at[j], m_recv.at[j],
@@ -179,11 +173,14 @@
                 turned[2 * d + r:2 * d + r + 1, :] = wanted[pl.ds(owner_of(d, r), 1), :]
         turned[...] = turned[...].T
 
-    def chunk(s, q):
-        return wbuf.at[s, pl.ds(q * QD, QD)]
-
-    def y_copy(q, device):
-        return remote(chunk(0, q), chunk(0, q), y_send.at[q], y_recv.at[q], device)
+    def chunk(s, r):
+        return wbuf.at[s, pl.ds(r * PART, PART)]
+
+    def y_copy(r, to, way):
+        return remote(chunk(0, r), chunk(0, to), y_send.at[r, way], y_recv.at[to], (up_y, down_y)[way])
+
+    keeper_sends = (((0, 0, 0), (0, 1, 1)), ((1, 2, 0),), ((2, 3, 1),), ())
+    other_sends = (((0, 1, 0),), ((1, 2, 1),), ((2, 3, 0),), ())
 
     def zp(s, q):
         return remote(chunk(s, q), chunk(s + 1, q), zp_send.at[s, q], zp_recv.at[s, q], up_z)
@@ -191,45 +188,36 @@
     def zm(s, q):
         return remote(chunk((8 - s) % 8, q), chunk(7 - s, q), zm_send.at[s, q], zm_recv.at[s, q], down_z)
 
-    def p_wait(i):
-        remote(w_in, wbuf.at[0, pl.ds(i * PIECE, PIECE)], p_send.at[0], p_recv.at[i], right).wait_recv()
-
     def sends_p(s, q):
-        return s < 3 or (s == 3 and q < NQ // 2)
+        return s < 3 or (s == 3 and q < NK // 2)
 
     def sends_m(s, q):
-        return s < 3 or (s == 3 and q >= NQ // 2)
+        return s < 3 or (s == 3 and q >= NK // 2)
 
     events = []
 
-    def ev_y(q):
-        @pl.when(dy == 0)
+    def ev_part(r):
+        @pl.when(keeper)
         def _():
-            for i in range(q * QD // PIECE, (q + 1) * QD // PIECE):
-                @pl.when(me8 == i)
-                def _():
-                    own_shard().wait()
-
-                @pl.when(me8 != i)
-                def _():
-                    p_wait(i)
-            y_copy(q, up_y).start()
-            remote(chunk(0, q), chunk(0, q), y_send.at[NQ + q], y_recv.at[q], down_y).start()
-
-        @pl.when(dy != 0)
+            if r == 0:
+                own_shard().wait()
+                for i in range(1, 8):
+                    source = lax.rem(me8 + i, 8)
+                    remote(flipped.at[pl.ds(0, PART)], wbuf.at[0, pl.ds(0, PART), pl.ds(0, PIECE)],
+                           p_send.at[0], p_recv.at[source], right).wait_recv()
+            else:
+                y_copy(r, r, 0).wait_recv()
+            for send in keeper_sends[r]:
+                y_copy(*send).start()
+
+        @pl.when(jnp.logical_not(keeper))
         def _():
-            y_copy(q, up_y).wait_recv()
-
-        @pl.when((dy >= 1) & (dy <= 3))
-        def _():
-            y_copy(q, up_y).start()
-
-        @pl.when(dy >= 6)
-        def _():
-            y_copy(q, down_y).start()
-
-        zp(0, q).start()
-        zm(0, q).start()
+            y_copy(r, r, 0).wait_recv()
+            for send in other_sends[r]:
+                y_copy(*send).start()
+
+        zp(0, r).start()
+        zm(0, r).start()
 
     def ev_zp(s, q):
         zp(s, q).wait_recv()
@@ -240,6 +228,10 @@
         zm(s, q).wait_recv()
         if sends_m(s + 1, q):
             zm(s + 1, q).start()
+
+    def ev_rows(n):
+        x_right(n).start()
+        x_left(NR - 1 - n).start()
 
     def ev_right(i):
         x_right(i).wait_recv()
@@ -264,28 +256,20 @@
         f_left_copy(i).wait_recv()
         sib(2, i).start()
 
-    wt = 2.15 * QD / 128
-    xt = 11.5 * RC / 32
-    for q in range(NQ):
-        events.append((9 + wt * q, ev_y, (q,)))
-    n = 0
-    for s in range(4):
-        for q in range(NQ):
+    for r, t in enumerate((6, 13, 15, 22)):
+        events.append((t, ev_part, (r,)))
+    for s, times in enumerate(((14, 18, 24, 29), (33, 37, 41, 45), (50, 54, 58, 62), (66, 67, 68, 69))):
+        for q, t in enumerate(times):
             if sends_p(s, q):
-                events.append((11 + wt * (n + 1), ev_zp, (s, q)))
-                n += 1
-    n = 0
-    for s in range(4):
-        for q in range(NQ):
+                events.append((t, ev_zp, (s, q)))
             if sends_m(s, q):
-                events.append((11 + wt * (n + 1), ev_zm, (s, q)))
-                n += 1
-    for i in range(NR):
-        events.append((4 + xt * (i + 1), ev_right, (i,)))
-        events.append((4 + xt * (i + 1), ev_left, (NR - 1 - i,)))
-    for i in range(NR // 2):
-        events.append((4 + xt * (NR + i + 1), ev_opp_right, (i,)))
-        events.append((4 + xt * (NR + i + 1), ev_opp_left, (NR - 1 - i,)))
+                events.append((t, ev_zm, (s, q)))
+    for i, t in enumerate((25, 34, 45.5, 58.5)):
+        events.append((t, ev_right, (i,)))
+        events.append((t, ev_left, (NR - 1 - i,)))
+    for i, t in enumerate((65.8, 74)):
+        events.append((t, ev_opp_right, (i,)))
+        events.append((t, ev_opp_left, (NR - 1 - i,)))
 
     def sib_wait(d):
         for i in range(NR):
@@ -296,51 +280,71 @@
             for s in sets:
                 start = pl.multiple_of(lax.rem(z - s + NZ, NZ) * DEPTH, DEPTH)
                 for r in range(2):
-                    part = jnp.dot(xbuf[d, r, :, pl.ds(start, DEPTH)], wbuf[s],
-                                   preferred_element_type=jnp.float32)
+                    part = lax.dot_general(xbuf[d, r, :, pl.ds(start, DEPTH)], wbuf[s], (((1,), (1,)), ((), ())),
+                                           preferred_element_type=jnp.float32)
                     if first and s == sets[0]:
                         acc[d, r] = part
                     else:
                         acc[d, r] += part
 
+    lane = lax.broadcasted_iota(jnp.int32, (1, COLS), 1)
+    column = lane
+    for r, (kept, other) in enumerate(((0, 7), (6, 1), (2, 5), (4, 3))):
+        block = lax.rem(y + jnp.where(keeper, kept, other), NY)
+        column = jnp.where(lane >= r * PART, block * COLS + x * PART + lane - r * PART, column)
+    column = column.astype(jnp.float32)
+    place = lax.broadcasted_iota(jnp.int32, (ROWS, 128), 1)
+
+    def note_statistics(ds, fresh):
+        gathered = jnp.zeros((ROWS, 128), jnp.float32) if fresh else noted[...]
+        for d in ds:
+            for r in range(2):
+                n = 2 * d + r
+                logits = acc[d, r]
+                largest = jnp.max(logits, axis=1, keepdims=True)
+                exp_total = jnp.sum(jnp.exp(logits - largest), axis=1, keepdims=True)
+                target = jnp.sum(jnp.where(column == turned[:, n:n + 1], logits, 0.0), axis=1, keepdims=True)
+                for which, v in enumerate((largest, exp_total, target)):
+                    gathered = jnp.where(place == 8 * which + n, v, gathered)
+        noted[...] = gathered
+
+    early = (0, 1, 7, 2, 6)
+
     def stage_a():
         sib_wait(0)
-        multiply((0,), (0, 1, 7), True)
+        multiply((0,), early, True)
 
     def stage_b():
         sib_wait(1)
         sib_wait(3)
-        multiply((1, 3), (0, 1, 7), True)
-        multiply((0, 1, 3), (2, 6))
+        multiply((1, 3), early, True)
 
     def stage_c():
         multiply((0, 1, 3), (3, 5))
 
-    events.append((11 + wt * 2 * NQ + 0.5, stage_a, ()))
-    events.append((11 + wt * 3 * NQ + 0.6, stage_b, ()))
-    events.append((11 + wt * 3.5 * NQ - wt, stage_c, ()))
-    events += [(6, ev_targets, ()), (16, ev_near, ()), (22, ev_wanted, ())]
+    def stage_d():
+        multiply((0, 1, 3), (4,))
+        note_statistics((0, 1, 3), True)
+
+    events += [(47, stage_a, ()), (59, stage_b, ()), (64, stage_c, ()), (70, stage_d, ())]
+    events += [(5.5, ev_near, ()), (40, ev_wanted, ())]
+    events += [(5.6, ev_rows, (n,)) for n in range(NR // 2, NR)]
     events.sort(key=lambda e: e[0])
 
+    ev_targets()
+    for n in range(NR // 2):
+        for i in (n, NR - 1 - n):
+            raw_copy(i).wait()
+            normalise(i)
+        ev_rows(n)
+    for i in range(NR):
+        sib(0, i).start()
     for _, go, given in events:
         go(*given)
     sib_wait(2)
-    multiply((0, 1, 3), (4,))
     multiply((2,), tuple(range(8)), True)
-
-    column = (lax.broadcasted_iota(jnp.int32, (ROWS, COLS), 1) + me8 * COLS).astype(jnp.float32)
-    place = lax.broadcasted_iota(jnp.int32, (ROWS, 128), 1)
-    gathered = jnp.zeros((ROWS, 128), jnp.float32)
-    for d in range(4):
-        for r in range(2):
-            n = 2 * d + r
-            logits = acc[d, r]
-            largest = jnp.max(logits, axis=1, keepdims=True)
-            exp_total = jnp.sum(jnp.exp(logits - largest), axis=1, keepdims=True)
-            target = jnp.sum(jnp.where(column == turned[:, n:n + 1], logits, 0.0), axis=1, keepdims=True)
-            for which, v in enumerate((largest, exp_total, target)):
-                gathered = jnp.where(place == 8 * which + n, v, gathered)
-    turned[...] = gathered.T
+    note_statistics((2,), False)
+    turned[...] = noted[...].T
     for d in range(4):
         for r in range(2):
             for which in range(3):
@@ -381,20 +385,24 @@
         result = result + jnp.sum(jnp.where(hits[k] > 0.5, value, 0.0), axis=0, keepdims=True)
     out_ref[...] = result
 
-    @pl.when(dy != 0)
+    for step in (1, 2, 3):
+        shard_copy(step).wait_send()
+
+    @pl.when(jnp.logical_not(keeper))
     def _():
-        shard_copy().wait_send()
-
-    for q in range(NQ):
-        @pl.when((dy <= 3) | (dy >= 6))
-        def _():
-            y_copy(q, up_y).wait_send()
-
-        @pl.when(dy == 0)
-        def _():
-            remote(chunk(0, q), chunk(0, q), y_send.at[NQ + q], y_recv.at[q], down_y).wait_send()
+        shard_copy(0).wait_send()
+        for sends in other_sends:
+            for send in sends:
+                y_copy(*send).wait_send()
+
+    @pl.when(keeper)
+    def _():
+        for sends in keeper_sends:
+            for send in sends:
+                y_copy(*send).wait_send()
+
     for s in range(4):
-        for q in range(NQ):
+        for q in range(NK):
             if sends_p(s, q):
                 zp(s, q).wait_send()
             if sends_m(s, q):
@@ -424,20 +432,21 @@
     log_probs = pl.pallas_call(
         kernel,
         out_shape=jax.ShapeDtypeStruct((1, 64), f32),
-        in_specs=[hbm, hbm, vmem, vmem, vmem],
+        in_specs=[hbm, vmem, vmem, vmem, vmem],
         out_specs=vmem,
         scratch_shapes=[
             pltpu.VMEM((ROWS, FEATURES), jnp.bfloat16),
+            pltpu.VMEM((COLS, PIECE), jnp.bfloat16),
             pltpu.VMEM((4, 2, ROWS, FEATURES), jnp.bfloat16),
-            pltpu.VMEM((NZ, DEPTH, COLS), jnp.bfloat16),
+            pltpu.VMEM((NZ, COLS, DEPTH), jnp.bfloat16),
             pltpu.VMEM((4, 2, ROWS, COLS), f32),
             pltpu.VMEM((NZ, *tile), f32), pltpu.VMEM((NZ, *tile), f32), pltpu.VMEM((8, *tile), f32),
-            pltpu.VMEM((2, 64, 64), f32), pltpu.VMEM(tile, f32), pltpu.VMEM((128, 128), f32),
+            pltpu.VMEM((2, 64, 64), f32), pltpu.VMEM(tile, f32), pltpu.VMEM((128, 128), f32), pltpu.VMEM((128, 128), f32),
             pltpu.VMEM((3, *tile), f32), pltpu.VMEM((8, 3, *tile), f32),
             pltpu.VMEM(tile, f32), pltpu.VMEM((NZ, *tile), f32),
             dma((NR,)), dma((8,)), dma((8,)), dma((8,)), dma((8,)), dma((8,)), dma((8,)), dma((8,)), dma((8,)),
-            dma((2 * NQ,)), dma((NQ,)), dma((1,)), dma((8,)), dma((1,)),
-            dma((4, NQ)), dma((4, NQ)), dma((4, NQ)), dma((4, NQ)),
+            dma((NK, 2)), dma((NK,)), dma((4,)), dma((8,)), dma((1,)),
+            dma((4, NK)), dma((4, NK)), dma((4, NK)), dma((4, NK)),
             dma((2 * NR,)), dma((2 * NR,)), dma((2 * NR,)), dma((2 * NR,)),
             dma((4, NR)), dma((4, NR)),
         ],

time: 131 us -> 107 us (0.82); the launches traced: 129 us -> 107 us
  Pallas kernels: 125 us -> 103 us
    pallas_call x1, Pallas kernels: 125 us -> 103 us  [body(): pl.pallas_call(kernel, out_shape=jax.ShapeDtypeStruct((1, 64), f32), in_s...]
where the time goes in v3:
time: 107 us
  Pallas kernels  103 us (96%)
  local copies, waits for them, and re-layouts  3.31 us (3%)
    pallas_call x1, Pallas kernels, body(): pl.pallas_call(kernel, out_shape=jax.ShapeDtypeStruct((1, 64), f32), in_s...  103 us
    reshape x1, local copies, waits for them, and re-layouts, body(): rows = lax.optimization_barrier(rollout_rows.reshape(ROWS, FEATURES))  2.78 us

profile of v3, /device:TPU:1, one launch (start us, length us, event | category | flops | bytes accessed | tf_op | source)
XLA Modules:
  0.0 106.7 jit_solution(9512570357457569745)
XLA Ops:
  0.0 0.0 copy-start
  0.0 0.0 copy-start.1
  0.0 0.0 copy-start.2
  0.0 0.0 copy-start.3
  0.0 2.8 %reshape.9.x_in = bf16[128,8192]{1,0:T(8,128)(2,1)S(1)} reshape(bf16[1,1,64,2,8192]{4,3,2,1,0:T(2,128)(2,1)} %param.5) | data formatting | bytes 4194304 | tf_op jit(solution)/shard_map/reshape | solution.py:426
  2.8 0.0 copy-done
  2.8 0.0 copy-done.1
  2.8 0.0 copy-done.2
  2.8 0.0 copy-done.3
  2.8 103.3 %shard_map.55 = f32[1,64]{1,0:T(1,128)S(1)} custom-call(bf16[128,8192]{1,0:T(8,128)(2,1)S(1)} %reshape.9.x_in, bf16[128,384]{1,0:T(8,128)(2,1)S(1)} %copy-done, s32[1,64]{1,0:T(1,128)S(1)} %bitcast.4, s32[1,8,64]{2,1,0:T(8,128)S(1)} %copy-done.2, f32[1,8192]{1,0:T(1,128)S(1)} %bitcast.3), custom_call_target="tpu_custom_call" | custom-call | flops 6442450944 | bytes 8388608 | tf_op jit(solution)/shard_map/pallas_call | solution.py:432
  106.1 0.5 copy.7
Async XLA Ops:
  0.0 2.8 %copy-start = (bf16[128,384]{1,0:T(8,128)(2,1)S(1)}, bf16[128,384]{1,0:T(8,128)(2,1)}, u32[]{:S(2)}) copy-start(bf16[128,384]{1,0:T(8,128)(2,1)} %w_in.1) | copy-start | bytes 294916
  0.0 2.8 %copy-start.1 = (f32[8192]{0:T(1024)S(1)}, f32[8192]{0:T(1024)}, u32[]{:S(2)}) copy-start(f32[8192]{0:T(1024)} %param.8) | copy-start | bytes 98308
  0.0 2.8 %copy-start.2 = (s32[1,8,64]{2,1,0:T(8,128)S(1)}, s32[1,8,64]{2,1,0:T(8,128)}, u32[]{:S(2)}) copy-start(s32[1,8,64]{2,1,0:T(8,128)} %targets_ref.1) | copy-start | bytes 6148
  0.0 2.8 %copy-start.3 = (s32[1,1,64]{2,1,0:T(1,128)S(1)}, s32[1,1,64]{2,1,0:T(1,128)}, u32[]{:S(2)}) copy-start(s32[1,1,64]{2,1,0:T(1,128)} %param.6) | copy-start | bytes 772

commit v4 on v3

--- a/solution.py
+++ b/solution.py
@@ -43,7 +43,7 @@
     keeper = lax.rem(y, 2) == c
 
     def raw_copy(i):
-        return pltpu.make_async_copy(rows(x_in, i), rows(raw, i), raw_sem.at[i])
+        return pltpu.make_async_copy(x_in.at[pl.ds(i * RC // 2, RC // 2)], raw.at[pl.ds(i * RC // 2, RC // 2)], raw_sem.at[i])
 
     def rows(ref, i):
         return ref.at[pl.ds(i * RC, RC)]
@@ -101,9 +101,13 @@
     def normalise(i):
         for b in range(i * RC, (i + 1) * RC, 16):
             here = pl.ds(b, 16)
+            pairs = pl.ds(b // 2, 8)
 
             def add(j, total):
-                v = raw[here, pl.ds(pl.multiple_of(j * 1024, 1024), 1024)].astype(jnp.float32)
+                lanes = pl.ds(pl.multiple_of(j * 1024, 1024), 1024)
+                v = raw[pairs, :, lanes].reshape(16, 1024)
+                xbuf[0, 0, here, lanes] = v
+                v = v.astype(jnp.float32)
                 v = v * v
                 for n in range(8):
                     total = total + v[:, n * 128:(n + 1) * 128]
@@ -114,7 +118,7 @@
 
             def put(j, carry):
                 lanes = pl.ds(pl.multiple_of(j * 1024, 1024), 1024)
-                v = raw[here, lanes].astype(jnp.float32)
+                v = xbuf[0, 0, here, lanes].astype(jnp.float32)
                 xbuf[0, 0, here, lanes] = (v * scaling * gain_ref[:, lanes]).astype(jnp.bfloat16)
                 return carry
 
@@ -267,7 +271,7 @@
     for i, t in enumerate((25, 34, 45.5, 58.5)):
         events.append((t, ev_right, (i,)))
         events.append((t, ev_left, (NR - 1 - i,)))
-    for i, t in enumerate((65.8, 74)):
+    for i, t in enumerate((65.8, 69.5)):
         events.append((t, ev_opp_right, (i,)))
         events.append((t, ev_opp_left, (NR - 1 - i,)))
 
@@ -324,21 +328,33 @@
 
     def stage_d():
         multiply((0, 1, 3), (4,))
+
+    def stage_e():
         note_statistics((0, 1, 3), True)
 
-    events += [(47, stage_a, ()), (59, stage_b, ()), (64, stage_c, ()), (70, stage_d, ())]
-    events += [(5.5, ev_near, ()), (40, ev_wanted, ())]
-    events += [(5.6, ev_rows, (n,)) for n in range(NR // 2, NR)]
+    events += [(47, stage_a, ()), (59, stage_b, ()), (64, stage_c, ()), (70, stage_d, ()), (75, stage_e, ())]
+    def ev_rest():
+        ev_normed(1)
+        x_right(1).start()
+        ev_normed(2)
+        x_left(2).start()
+        ev_rows(2)
+        ev_rows(3)
+        for i in range(NR):
+            sib(0, i).start()
+
+    events += [(6.1, ev_near, ()), (40, ev_wanted, ()), (6.2, ev_rest, ())]
     events.sort(key=lambda e: e[0])
 
+    def ev_normed(i):
+        raw_copy(i).wait()
+        normalise(i)
+
+    ev_normed(0)
+    x_right(0).start()
+    ev_normed(NR - 1)
+    x_left(NR - 1).start()
     ev_targets()
-    for n in range(NR // 2):
-        for i in (n, NR - 1 - n):
-            raw_copy(i).wait()
-            normalise(i)
-        ev_rows(n)
-    for i in range(NR):
-        sib(0, i).start()
     for _, go, given in events:
         go(*given)
     sib_wait(2)
@@ -423,7 +439,7 @@
 
 
 def body(rollout_rows, counts, targets, final_gain, lm_head):
-    rows = lax.optimization_barrier(rollout_rows.reshape(ROWS, FEATURES))
+    rows = rollout_rows.reshape(64, 2, FEATURES)
     dma = pltpu.SemaphoreType.DMA
     vmem = pl.BlockSpec(memory_space=pltpu.VMEM)
     hbm = pl.BlockSpec(memory_space=pl.ANY)
@@ -435,7 +451,7 @@
         in_specs=[hbm, vmem, vmem, vmem, vmem],
         out_specs=vmem,
         scratch_shapes=[
-            pltpu.VMEM((ROWS, FEATURES), jnp.bfloat16),
+            pltpu.VMEM((64, 2, FEATURES), jnp.bfloat16),
             pltpu.VMEM((COLS, PIECE), jnp.bfloat16),
             pltpu.VMEM((4, 2, ROWS, FEATURES), jnp.bfloat16),
             pltpu.VMEM((NZ, COLS, DEPTH), jnp.bfloat16),
@@ -451,7 +467,7 @@
             dma((4, NR)), dma((4, NR)),
         ],
         compiler_params=pltpu.CompilerParams(
-            collective_id=0, has_side_effects=True, vmem_limit_bytes=48 * 2**20),
+            collective_id=0, has_side_effects=True, vmem_limit_bytes=60 * 2**20),
         cost_estimate=pl.CostEstimate(flops=2 * 1024 * COLS * FEATURES, bytes_accessed=8 * 2**20, transcendentals=0),
     )(rows, lm_head, counts[0], targets, final_gain.reshape(1, FEATURES))
     return log_probs.reshape(1, 1, 64)

time: 107 us -> 103 us (0.963)
  local copies, waits for them, and re-layouts: 3.31 us -> 1.19 us
  Pallas kernels: 103 us -> 101 us
    reshape x1 -> x0, local copies, waits for them, and re-layouts: 2.78 us -> none  [body(): rows = lax.optimization_barrier(rollout_rows.reshape(ROWS, FEATURES))]
    pallas_call x1, Pallas kernels: 103 us -> 101 us  [body(): pl.pallas_call(kernel, out_shape=jax.ShapeDtypeStruct((1, 64), f32), in_s...]
where the time goes in v4:
time: 103 us; the launch traced here: 102 us
  Pallas kernels  101 us (98%)
  local copies, waits for them, and re-layouts  1.19 us (1%)
    pallas_call x1, Pallas kernels, body(): pl.pallas_call(kernel, out_shape=jax.ShapeDtypeStruct((1, 64), f32), in_s...  101 us

profile of v4, /device:TPU:1, one launch (start us, length us, event | category | flops | bytes accessed | tf_op | source)
XLA Modules:
  0.0 102.5 jit_solution(5242593448325473427)
XLA Ops:
  0.0 101.3 %shard_map.55 = f32[1,64]{1,0:T(1,128)} custom-call(bf16[64,2,8192]{2,1,0:T(2,128)(2,1)} %bitcast.4, bf16[128,384]{1,0:T(8,128)(2,1)} %w_in.1, s32[1,64]{1,0:T(1,128)} %bitcast.6, s32[1,8,64]{2,1,0:T(8,128)} %targets_ref.1, f32[1,8192]{1,0:T(1,128)} %bitcast.5), custom_call_target="tpu_custom_call" | custom-call | flops 6442450944 | bytes 8388608 | tf_op jit(solution)/shard_map/pallas_call | solution.py:448
  101.3 1.2 %copy.7 = f32[1,1,64]{2,1,0:T(1,128)} copy(f32[1,1,64]{2,1,0:T(1,128)} %bitcast.7) | data formatting | bytes 512

commit v5 on v4

--- a/solution.py
+++ b/solution.py
@@ -18,7 +18,7 @@
 MESH = pl.DeviceIdType.MESH
 
 
-def kernel(x_in, w_in, counts_ref, targets_ref, gain_ref, out_ref, raw, flipped, xbuf, wbuf, acc,
+def kernel(x_in, w_hbm, counts_hbm, targets_hbm, gain_hbm, out_ref, w_in, counts_ref, targets_ref, gain_ref, in_sem, raw, flipped, xbuf, wbuf, acc,
            messages, near_targets, ring_targets, hits, wanted, turned, noted, stats, ring_stats, slot_out, slot_in,
            raw_sem, m_send, m_recv, t_send, t_recv, st_send, st_recv, lp_send, lp_recv, y_send, y_recv, p_send, p_recv, p_own,
            zp_send, zp_recv, zm_send, zm_recv, xr_send, xr_recv, xl_send, xl_recv,
@@ -48,8 +48,15 @@
     def rows(ref, i):
         return ref.at[pl.ds(i * RC, RC)]
 
-    for i in range(NR):
+    fetches = [pltpu.make_async_copy(src, dst, in_sem.at[n]) for n, (src, dst) in enumerate((
+        (w_hbm, w_in), (gain_hbm, gain_ref), (counts_hbm, counts_ref), (targets_hbm, targets_ref)))]
+    fetches[0].start()
+    raw_copy(0).start()
+    fetches[1].start()
+    for i in range(1, NR):
         raw_copy(i).start()
+    fetches[2].start()
+    fetches[3].start()
 
     barrier = pltpu.get_barrier_semaphore()
     for step in range(1, 8):
@@ -57,6 +64,7 @@
         pl.semaphore_signal(barrier, inc=1, device_id=(y, lax.rem(dp + 8 * step, 64)), device_id_type=MESH)
     for other in (up_y, down_y):
         pl.semaphore_signal(barrier, inc=1, device_id=other, device_id_type=MESH)
+    fetches[0].wait()
     flipped[...] = w_in[...].astype(jnp.float32).T.astype(jnp.bfloat16)
     pl.semaphore_wait(barrier, 16)
 
@@ -283,13 +291,13 @@
         for d in ds:
             for s in sets:
                 start = pl.multiple_of(lax.rem(z - s + NZ, NZ) * DEPTH, DEPTH)
-                for r in range(2):
-                    part = lax.dot_general(xbuf[d, r, :, pl.ds(start, DEPTH)], wbuf[s], (((1,), (1,)), ((), ())),
-                                           preferred_element_type=jnp.float32)
-                    if first and s == sets[0]:
-                        acc[d, r] = part
-                    else:
-                        acc[d, r] += part
+                both = xbuf[d, :, :, pl.ds(start, DEPTH)].reshape(2 * ROWS, DEPTH)
+                part = lax.dot_general(both, wbuf[s], (((1,), (1,)), ((), ())), preferred_element_type=jnp.float32)
+                part = part.reshape(2, ROWS, COLS)
+                if first and s == sets[0]:
+                    acc[d] = part
+                else:
+                    acc[d] += part
 
     lane = lax.broadcasted_iota(jnp.int32, (1, COLS), 1)
     column = lane
@@ -332,7 +340,7 @@
     def stage_e():
         note_statistics((0, 1, 3), True)
 
-    events += [(47, stage_a, ()), (59, stage_b, ()), (64, stage_c, ()), (70, stage_d, ()), (75, stage_e, ())]
+    events += [(47, stage_a, ()), (62.5, stage_b, ()), (64, stage_c, ()), (70, stage_d, ()), (75, stage_e, ())]
     def ev_rest():
         ev_normed(1)
         x_right(1).start()
@@ -350,10 +358,13 @@
         raw_copy(i).wait()
         normalise(i)
 
+    fetches[1].wait()
     ev_normed(0)
     x_right(0).start()
     ev_normed(NR - 1)
     x_left(NR - 1).start()
+    fetches[2].wait()
+    fetches[3].wait()
     ev_targets()
     for _, go, given in events:
         go(*given)
@@ -370,7 +381,7 @@
     def st_copy(j):
         return remote(stats, ring_stats.at[j], st_send.at[j], st_recv.at[j], ring(j))
 
-    for j in range(1, 8):
+    for j in (4, 3, 5, 2, 6, 1, 7):
         st_copy(j).start()
     for j in range(1, 8):
         st_copy(j).wait_recv()
@@ -388,7 +399,7 @@
     def lp_copy(j):
         return remote(slot_out, slot_in.at[z], lp_send.at[j], lp_recv.at[j], (y, lax.rem(dp + 8 * j, 64)))
 
-    for j in range(1, 8):
+    for j in (4, 3, 5, 2, 6, 1, 7):
         lp_copy(j).start()
     slot_in[z] = slot_out[...]
     for j in range(1, 8):
@@ -448,9 +459,11 @@
     log_probs = pl.pallas_call(
         kernel,
         out_shape=jax.ShapeDtypeStruct((1, 64), f32),
-        in_specs=[hbm, vmem, vmem, vmem, vmem],
+        in_specs=[hbm] * 5,
         out_specs=vmem,
         scratch_shapes=[
+            pltpu.VMEM((PIECE, COLS), jnp.bfloat16), pltpu.VMEM((1, 64), jnp.int32), pltpu.VMEM((1, NY, 64), jnp.int32),
+            pltpu.VMEM((1, FEATURES), f32), dma((4,)),
             pltpu.VMEM((64, 2, FEATURES), jnp.bfloat16),
             pltpu.VMEM((COLS, PIECE), jnp.bfloat16),
             pltpu.VMEM((4, 2, ROWS, FEATURES), jnp.bfloat16),

time: 103 us -> 100 us (0.971)
  Pallas kernels: 101 us -> 98.6 us
    pallas_call x1, Pallas kernels: 101 us -> 98.6 us  [body(): pl.pallas_call(kernel, out_shape=jax.ShapeDtypeStruct((1, 64), f32), in_s...]
where the time goes in v5:
time: 100 us; the launch traced here: 99.8 us
  Pallas kernels  98.6 us (99%)
  local copies, waits for them, and re-layouts  1.19 us (1%)
    pallas_call x1, Pallas kernels, body(): pl.pallas_call(kernel, out_shape=jax.ShapeDtypeStruct((1, 64), f32), in_s...  98.6 us

profile of v5, /device:TPU:1, one launch (start us, length us, event | category | flops | bytes accessed | tf_op | source)
XLA Modules:
  0.0 99.8 jit_solution(7008181284856611826)
XLA Ops:
  0.0 98.6 %shard_map.55 = f32[1,64]{1,0:T(1,128)} custom-call(bf16[64,2,8192]{2,1,0:T(2,128)(2,1)} %bitcast.4, bf16[128,384]{1,0:T(8,128)(2,1)} %w_hbm.1, s32[1,64]{1,0:T(1,128)} %bitcast.6, s32[1,8,64]{2,1,0:T(8,128)} %targets_hbm.1, f32[1,8192]{1,0:T(1,128)} %bitcast.5), custom_call_target="tpu_custom_call" | custom-call | flops 6442450944 | bytes 8388608 | tf_op jit(solution)/shard_map/pallas_call | solution.py:459
  98.6 1.2 %copy.7 = f32[1,1,64]{2,1,0:T(1,128)} copy(f32[1,1,64]{2,1,0:T(1,128)} %bitcast.7) | data formatting | bytes 512

commit v6 on v5

--- a/solution.py
+++ b/solution.py
@@ -66,46 +66,6 @@
         pl.semaphore_signal(barrier, inc=1, device_id=other, device_id_type=MESH)
     fetches[0].wait()
     flipped[...] = w_in[...].astype(jnp.float32).T.astype(jnp.bfloat16)
-    pl.semaphore_wait(barrier, 16)
-
-    def remote(src, dst, send, recv, device):
-        return pltpu.make_async_remote_copy(
-            src_ref=src, dst_ref=dst, send_sem=send, recv_sem=recv, device_id=device, device_id_type=MESH)
-
-    def shard_copy(step):
-        other = lax.rem(x + step, NX)
-        return remote(flipped.at[pl.ds(pl.multiple_of(other * PART, PART), PART)],
-                      wbuf.at[0, pl.ds(0, PART), pl.ds(pl.multiple_of(me8 * PIECE, PIECE), PIECE)],
-                      p_send.at[step], p_recv.at[me8], (y, at(z, other, lax.rem(y, 2))))
-
-    def own_shard():
-        return pltpu.make_async_copy(
-            flipped.at[pl.ds(pl.multiple_of(x * PART, PART), PART)],
-            wbuf.at[0, pl.ds(0, PART), pl.ds(pl.multiple_of(me8 * PIECE, PIECE), PIECE)], p_own.at[0])
-
-    for step in (2, 1, 3):
-        shard_copy(step).start()
-
-    @pl.when(keeper)
-    def _():
-        own_shard().start()
-
-    @pl.when(jnp.logical_not(keeper))
-    def _():
-        shard_copy(0).start()
-
-    def x_right(i):
-        return remote(rows(xbuf.at[0, 0], i), rows(xbuf.at[1, 0], i), xr_send.at[i], xr_recv.at[i], right)
-
-    def x_left(i):
-        return remote(rows(xbuf.at[0, 0], i), rows(xbuf.at[3, 0], i), xl_send.at[i], xl_recv.at[i], left)
-
-    def f_right(i):
-        return remote(rows(xbuf.at[1, 0], i), rows(xbuf.at[2, 0], i), xr_send.at[NR + i], xr_recv.at[NR + i], right)
-
-    def sib(d, i):
-        return remote(rows(xbuf.at[d, 0], i), rows(xbuf.at[d, 1], i), s_send.at[d, i], s_recv.at[d, i], sibling)
-
     def normalise(i):
         for b in range(i * RC, (i + 1) * RC, 16):
             here = pl.ds(b, 16)
@@ -131,6 +91,56 @@
                 return carry
 
             lax.fori_loop(0, FEATURES // 1024, put, 0)
+
+    def ev_normed(i):
+        raw_copy(i).wait()
+        normalise(i)
+
+    fetches[1].wait()
+    ev_normed(0)
+    ev_normed(NR - 1)
+    pl.semaphore_wait(barrier, 16)
+
+    def remote(src, dst, send, recv, device):
+        return pltpu.make_async_remote_copy(
+            src_ref=src, dst_ref=dst, send_sem=send, recv_sem=recv, device_id=device, device_id_type=MESH)
+
+    def shard_copy(step):
+        other = lax.rem(x + step, NX)
+        return remote(flipped.at[pl.ds(pl.multiple_of(other * PART, PART), PART)],
+                      wbuf.at[0, pl.ds(0, PART), pl.ds(pl.multiple_of(me8 * PIECE, PIECE), PIECE)],
+                      p_send.at[step], p_recv.at[me8], (y, at(z, other, lax.rem(y, 2))))
+
+    def own_shard():
+        return pltpu.make_async_copy(
+            flipped.at[pl.ds(pl.multiple_of(x * PART, PART), PART)],
+            wbuf.at[0, pl.ds(0, PART), pl.ds(pl.multiple_of(me8 * PIECE, PIECE), PIECE)], p_own.at[0])
+
+    for step in (2, 1, 3):
+        shard_copy(step).start()
+
+    @pl.when(keeper)
+    def _():
+        own_shard().start()
+
+    @pl.when(jnp.logical_not(keeper))
+    def _():
+        shard_copy(0).start()
+
+    def x_right(i):
+        return remote(rows(xbuf.at[0, 0], i), rows(xbuf.at[1, 0], i), xr_send.at[i], xr_recv.at[i], right)
+
+    def x_left(i):
+        return remote(rows(xbuf.at[0, 0], i), rows(xbuf.at[3, 0], i), xl_send.at[i], xl_recv.at[i], left)
+
+    def f_right(i):
+        return remote(rows(xbuf.at[1, 0], i), rows(xbuf.at[2, 0], i), xr_send.at[NR + i], xr_recv.at[NR + i], right)
+
+    def sib(d, i):
+        return remote(rows(xbuf.at[d, 0], i), rows(xbuf.at[d, 1], i), s_send.at[d, i], s_recv.at[d, i], sibling)
+
+    x_right(0).start()
+    x_left(NR - 1).start()
 
     def m_copy(j):
         return remote(messages.at[lax.rem(z + j, NZ)], near_targets.at[j], m_send.at[j], m_recv.at[j],
@@ -354,15 +364,6 @@
     events += [(6.1, ev_near, ()), (40, ev_wanted, ()), (6.2, ev_rest, ())]
     events.sort(key=lambda e: e[0])
 
-    def ev_normed(i):
-        raw_copy(i).wait()
-        normalise(i)
-
-    fetches[1].wait()
-    ev_normed(0)
-    x_right(0).start()
-    ev_normed(NR - 1)
-    x_left(NR - 1).start()
     fetches[2].wait()
     fetches[3].wait()
     ev_targets()

time: 100 us -> 99.3 us (level)
  no operation moved by 1% of the time
where the time goes in v6:
time: 99.3 us; the launch traced here: 99.2 us
  Pallas kernels  98 us (99%)
  local copies, waits for them, and re-layouts  1.19 us (1%)
    pallas_call x1, Pallas kernels, body(): pl.pallas_call(kernel, out_shape=jax.ShapeDtypeStruct((1, 64), f32), in_s...  98 us

profile of v6, /device:TPU:1, one launch (start us, length us, event | category | flops | bytes accessed | tf_op | source)
XLA Modules:
  0.0 99.2 jit_solution(11429548967344294782)
XLA Ops:
  0.0 98.0 %shard_map.55 = f32[1,64]{1,0:T(1,128)} custom-call(bf16[64,2,8192]{2,1,0:T(2,128)(2,1)} %bitcast.4, bf16[128,384]{1,0:T(8,128)(2,1)} %w_hbm.1, s32[1,64]{1,0:T(1,128)} %bitcast.6, s32[1,8,64]{2,1,0:T(8,128)} %targets_hbm.1, f32[1,8192]{1,0:T(1,128)} %bitcast.5), custom_call_target="tpu_custom_call" | custom-call | flops 6442450944 | bytes 8388608 | tf_op jit(solution)/shard_map/pallas_call | solution.py:460
  98.0 1.2 %copy.7 = f32[1,1,64]{2,1,0:T(1,128)} copy(f32[1,1,64]{2,1,0:T(1,128)} %bitcast.7) | data formatting | bytes 512
